TPU v7x, 32 devices: a whole 2x2x4 slice. The times are simulated.
32 devices in a mesh: img: 8 (over z, y), band: 4 (over x, core).
Axes of the slice: x: 2, y: 2, z: 4, core: 2. Of those that a mesh axis runs over, the one named last changes fastest.
Arguments:
- tokens: bfloat16 [64, 256, 768], P('img', 'band'), may hold values from -6 to 6
- cotangent: bfloat16 [64, 256, 768], P('img', 'band'), may hold values from -6 to 6
- grid_side: int32 [64], P('img'), may hold values from 10 to 16, as said below
- visible: int32 [64, 256], P('img'), may hold values from 0 to 1, as said below
- w_qkv: bfloat16 [768, 2304], replicated, may hold values from -0.21875 to 0.21875
- q_bias: float32 [768], replicated, may hold values from -3 to 3
- v_bias: float32 [768], replicated, may hold values from -3 to 3
- w_out: bfloat16 [768, 768], replicated, may hold values from -0.625 to 0.625
- b_out: float32 [768], replicated, may hold values from -2 to 2
- ln1_gain: float32 [768], replicated, may hold values from 0.1 to 1.9
- ln1_shift: float32 [768], replicated, may hold values from -2 to 2
- ln2_gain: float32 [768], replicated, may hold values from 0.1 to 1.9
- ln2_shift: float32 [768], replicated, may hold values from -2 to 2
- w_up: bfloat16 [768, 3072], replicated, may hold values from -0.21875 to 0.21875
- b_up: float32 [3072], replicated, may hold values from -3 to 3
- w_down: bfloat16 [3072, 768], replicated, may hold values from -0.15625 to 0.15625
- b_down: float32 [768], replicated, may hold values from -2 to 2
- scale_attn: float32 [768], replicated, may hold values from 0.3 to 1
- scale_mlp: float32 [768], replicated, may hold values from 0.3 to 1
Outputs:
- output: bfloat16 [64, 256, 768], P('img', 'band')
- input_grad: bfloat16 [64, 256, 768], P('img', 'band')
- grad_w_qkv: float32 [768, 2304], P('img')
- grad_q_bias: float32 [768], P('img')
- grad_v_bias: float32 [768], P('img')
- grad_w_out: float32 [768, 768], P('img')
- grad_b_out: float32 [768], P('img')
- grad_ln1_gain: float32 [768], P('img')
- grad_ln1_shift: float32 [768], P('img')
- grad_ln2_gain: float32 [768], P('img')
- grad_ln2_shift: float32 [768], P('img')
- grad_w_up: float32 [768, 3072], P('img')
- grad_b_up: float32 [3072], P('img')
- grad_w_down: float32 [3072, 768], P('img')
- grad_b_down: float32 [768], P('img')
- grad_scale_attn: float32 [768], P('img')
- grad_scale_mlp: float32 [768], P('img')
Inputs may be any that keep to these rules, and one draw needn't show every extreme that they name: `grid_side`: each grid side is 10, 14 or 16; in each aligned block of 8 images at least one has side 16. Slot 0 of every image is visible.
All inputs are finite; a program needn't handle non-finite values.
Results may differ from a plain program's by a relative error of at most 0.015.
Values may be sent and summed in bfloat16 or wider, within the bound.
No kernel may reach another device: no remote copies, remote signals or barrier semaphores. Data moves between devices by JAX's collectives and lax.ppermute only.
A program may use at most 128 MiB of HBM per device.

v0:
```python
import jax
import jax.numpy as jnp
from jax import lax
from jax.sharding import PartitionSpec as P

HEAD = 64
GRID = 16


NEG_BIG = -1e30
EPSILON = 1e-06


def layer_norm(entry, gain, shift):
    center = entry - jnp.mean(entry, -1, keepdims=True)
    spread = jnp.mean(center * center, -1, keepdims=True)
    return center * lax.rsqrt(spread + EPSILON) * gain + shift


def gelu_exact(entry):
    return jax.nn.gelu(entry, approximate=False)


def slot_mask(sides, count, first):
    index = first + jnp.arange(count, dtype=jnp.int32)
    row_pos = index // GRID
    col_pos = index % GRID
    return (row_pos[None, :] < sides[:, None]) & (col_pos[None, :] < sides[:, None])


def masked_scores(queries, key_rows, key_ok):
    factor = queries.shape[-1] ** (-0.5)
    scores = (
        jnp.einsum("qhe,khe->hqk", queries, key_rows, preferred_element_type=jnp.float32) * factor
    )
    return jnp.where(key_ok[None, None, :], scores, NEG_BIG)


def attend_one(items):
    queries, key_rows, values, key_ok = items
    scores = masked_scores(queries, key_rows, key_ok)
    row_top = jnp.max(scores, -1, keepdims=True)
    exponent = jnp.exp(scores - row_top)
    row_total = jnp.sum(exponent, -1, keepdims=True)
    weights = (exponent / row_total).astype(jnp.bfloat16)
    attended = jnp.einsum("hqk,khe->qhe", weights, values, preferred_element_type=jnp.float32)
    return (attended.astype(jnp.bfloat16), (row_top + jnp.log(row_total))[..., 0])


def attend_back(items):
    queries, key_rows, values, key_ok, log_total, grad_attended = items
    factor = queries.shape[-1] ** (-0.5)
    scores = masked_scores(queries, key_rows, key_ok)
    probs = jnp.exp(scores - log_total[..., None])
    grad_weights = jnp.einsum(
        "qhe,khe->hqk", grad_attended, values, preferred_element_type=jnp.float32
    )
    grad_scores = probs * (grad_weights - jnp.sum(probs * grad_weights, -1, keepdims=True))
    grad_scores = grad_scores.astype(jnp.bfloat16)
    grad_queries = (
        jnp.einsum("hqk,khe->qhe", grad_scores, key_rows, preferred_element_type=jnp.float32)
        * factor
    )
    grad_keys = (
        jnp.einsum("hqk,qhe->khe", grad_scores, queries, preferred_element_type=jnp.float32)
        * factor
    )
    grad_values = jnp.einsum(
        "hqk,qhe->khe",
        probs.astype(jnp.bfloat16),
        grad_attended,
        preferred_element_type=jnp.float32,
    )
    return (
        grad_queries.astype(jnp.bfloat16),
        grad_keys.astype(jnp.bfloat16),
        grad_values.astype(jnp.bfloat16),
    )


def shards(
    tokens,
    cotangent,
    grid_side,
    visible,
    w_qkv,
    q_bias,
    v_bias,
    w_out,
    b_out,
    ln1_gain,
    ln1_shift,
    ln2_gain,
    ln2_shift,
    w_up,
    b_up,
    w_down,
    b_down,
    scale_attn,
    scale_mlp,
):
    images, band_rows, model_width = tokens.shape
    band_count = lax.axis_size("band")
    slot_count = band_rows * band_count
    group_width = model_width // band_count
    group_heads = group_width // HEAD
    valid_f = slot_mask(grid_side, band_rows, lax.axis_index("band") * band_rows).astype(
        jnp.float32
    )[..., None]
    key_ok = slot_mask(grid_side, slot_count, 0) & (visible == 1)

    def split_groups(entry):
        return entry.reshape(images, band_rows, band_count, group_width)

    def as_heads(entry):
        return entry.reshape(images, slot_count, group_heads, HEAD)

    def join_groups(entry):
        return entry.reshape(images, slot_count, 1, group_width)

    def as_bands(entry):
        return entry.reshape(images, band_rows, model_width)

    inputs = tokens.astype(jnp.float32)
    normed, norm_one_pull = jax.vjp(layer_norm, inputs, ln1_gain, ln1_shift)
    normed_low = normed.astype(jnp.bfloat16)
    projected = jnp.einsum("nsd,de->nse", normed_low, w_qkv, preferred_element_type=jnp.float32)
    queries = (projected[..., :model_width] + q_bias).astype(jnp.bfloat16)
    key_rows = projected[..., model_width : 2 * model_width].astype(jnp.bfloat16)
    values = (projected[..., 2 * model_width :] + v_bias).astype(jnp.bfloat16)
    head_queries, head_keys, head_values = (
        lax.all_to_all(split_groups(queries), "band", split_axis=2, concat_axis=1, tiled=True),
        lax.all_to_all(split_groups(key_rows), "band", split_axis=2, concat_axis=1, tiled=True),
        lax.all_to_all(split_groups(values), "band", split_axis=2, concat_axis=1, tiled=True),
    )
    head_queries = as_heads(head_queries)
    head_keys = as_heads(head_keys)
    head_values = as_heads(head_values)
    attended, log_total = lax.map(attend_one, (head_queries, head_keys, head_values, key_ok))
    attended_bands = as_bands(
        lax.all_to_all(join_groups(attended), "band", split_axis=1, concat_axis=2, tiled=True)
    )
    branch_attn = (
        jnp.einsum("nsd,de->nse", attended_bands, w_out, preferred_element_type=jnp.float32) + b_out
    )
    middle = inputs + scale_attn * branch_attn
    normed_two, norm_two_pull = jax.vjp(layer_norm, middle, ln2_gain, ln2_shift)
    normed_two_low = normed_two.astype(jnp.bfloat16)
    hidden_pre = (
        jnp.einsum("nsd,df->nsf", normed_two_low, w_up, preferred_element_type=jnp.float32) + b_up
    )
    hidden_low = gelu_exact(hidden_pre).astype(jnp.bfloat16)
    branch_mlp = (
        jnp.einsum("nsf,fd->nsd", hidden_low, w_down, preferred_element_type=jnp.float32) + b_down
    )
    output = (valid_f * (middle + scale_mlp * branch_mlp)).astype(jnp.bfloat16)
    grad_top = valid_f * cotangent.astype(jnp.float32)
    grad_scale_mlp = jnp.sum(grad_top * branch_mlp, axis=(0, 1))
    grad_branch_mlp = (scale_mlp * grad_top).astype(jnp.bfloat16)
    grad_w_down = jnp.einsum(
        "nsf,nsd->fd", hidden_low, grad_branch_mlp, preferred_element_type=jnp.float32
    )
    grad_b_down = jnp.sum(grad_branch_mlp.astype(jnp.float32), axis=(0, 1))
    grad_hidden = jnp.einsum(
        "nsd,fd->nsf", grad_branch_mlp, w_down, preferred_element_type=jnp.float32
    )
    gelu_out, gelu_pull = jax.vjp(gelu_exact, hidden_pre)
    grad_pre = gelu_pull(grad_hidden)[0].astype(jnp.bfloat16)
    grad_w_up = jnp.einsum(
        "nsd,nsf->df", normed_two_low, grad_pre, preferred_element_type=jnp.float32
    )
    grad_b_up = jnp.sum(grad_pre.astype(jnp.float32), axis=(0, 1))
    grad_normed_two = jnp.einsum("nsf,df->nsd", grad_pre, w_up, preferred_element_type=jnp.float32)
    grad_from_norm, grad_ln2_gain, grad_ln2_shift = norm_two_pull(grad_normed_two)
    grad_middle = grad_top + grad_from_norm
    grad_scale_attn = jnp.sum(grad_middle * branch_attn, axis=(0, 1))
    grad_branch_attn = (scale_attn * grad_middle).astype(jnp.bfloat16)
    grad_w_out = jnp.einsum(
        "nsd,nse->de", attended_bands, grad_branch_attn, preferred_element_type=jnp.float32
    )
    grad_b_out = jnp.sum(grad_branch_attn.astype(jnp.float32), axis=(0, 1))
    grad_attended = jnp.einsum(
        "nse,de->nsd", grad_branch_attn, w_out, preferred_element_type=jnp.float32
    ).astype(jnp.bfloat16)
    head_grad = as_heads(
        lax.all_to_all(split_groups(grad_attended), "band", split_axis=2, concat_axis=1, tiled=True)
    )
    grad_q_heads, grad_k_heads, grad_v_heads = lax.map(
        attend_back, (head_queries, head_keys, head_values, key_ok, log_total, head_grad)
    )
    grad_queries, grad_keys, grad_values = (
        lax.all_to_all(join_groups(grad_q_heads), "band", split_axis=1, concat_axis=2, tiled=True),
        lax.all_to_all(join_groups(grad_k_heads), "band", split_axis=1, concat_axis=2, tiled=True),
        lax.all_to_all(join_groups(grad_v_heads), "band", split_axis=1, concat_axis=2, tiled=True),
    )
    grad_projected = jnp.concatenate(
        [as_bands(grad_queries), as_bands(grad_keys), as_bands(grad_values)], axis=-1
    )
    grad_w_qkv = jnp.einsum(
        "nsd,nse->de", normed_low, grad_projected, preferred_element_type=jnp.float32
    )
    grad_q_bias = jnp.sum(as_bands(grad_queries).astype(jnp.float32), axis=(0, 1))
    grad_v_bias = jnp.sum(as_bands(grad_values).astype(jnp.float32), axis=(0, 1))
    grad_normed = jnp.einsum(
        "nse,de->nsd", grad_projected, w_qkv, preferred_element_type=jnp.float32
    )
    grad_from_first, grad_ln1_gain, grad_ln1_shift = norm_one_pull(grad_normed)
    input_grad = (grad_middle + grad_from_first).astype(jnp.bfloat16)
    (
        part_w_qkv,
        part_q_bias,
        part_v_bias,
        part_w_out,
        part_b_out,
        part_ln1_gain,
        part_ln1_shift,
        part_ln2_gain,
        part_ln2_shift,
        part_w_up,
        part_b_up,
        part_w_down,
        part_b_down,
        part_scale_attn,
        part_scale_mlp,
    ) = (
        lax.psum_scatter(grad_w_qkv, "img", scatter_dimension=0, tiled=True),
        lax.psum_scatter(grad_q_bias, "img", scatter_dimension=0, tiled=True),
        lax.psum_scatter(grad_v_bias, "img", scatter_dimension=0, tiled=True),
        lax.psum_scatter(grad_w_out, "img", scatter_dimension=0, tiled=True),
        lax.psum_scatter(grad_b_out, "img", scatter_dimension=0, tiled=True),
        lax.psum_scatter(grad_ln1_gain, "img", scatter_dimension=0, tiled=True),
        lax.psum_scatter(grad_ln1_shift, "img", scatter_dimension=0, tiled=True),
        lax.psum_scatter(grad_ln2_gain, "img", scatter_dimension=0, tiled=True),
        lax.psum_scatter(grad_ln2_shift, "img", scatter_dimension=0, tiled=True),
        lax.psum_scatter(grad_w_up, "img", scatter_dimension=0, tiled=True),
        lax.psum_scatter(grad_b_up, "img", scatter_dimension=0, tiled=True),
        lax.psum_scatter(grad_w_down, "img", scatter_dimension=0, tiled=True),
        lax.psum_scatter(grad_b_down, "img", scatter_dimension=0, tiled=True),
        lax.psum_scatter(grad_scale_attn, "img", scatter_dimension=0, tiled=True),
        lax.psum_scatter(grad_scale_mlp, "img", scatter_dimension=0, tiled=True),
    )
    (
        grad_w_qkv,
        grad_q_bias,
        grad_v_bias,
        grad_w_out,
        grad_b_out,
        grad_ln1_gain,
        grad_ln1_shift,
        grad_ln2_gain,
        grad_ln2_shift,
        grad_w_up,
        grad_b_up,
        grad_w_down,
        grad_b_down,
        grad_scale_attn,
        grad_scale_mlp,
    ) = (
        lax.psum(part_w_qkv.astype(jnp.bfloat16), "band").astype(jnp.float32),
        lax.psum(part_q_bias.astype(jnp.bfloat16), "band").astype(jnp.float32),
        lax.psum(part_v_bias.astype(jnp.bfloat16), "band").astype(jnp.float32),
        lax.psum(part_w_out.astype(jnp.bfloat16), "band").astype(jnp.float32),
        lax.psum(part_b_out.astype(jnp.bfloat16), "band").astype(jnp.float32),
        lax.psum(part_ln1_gain.astype(jnp.bfloat16), "band").astype(jnp.float32),
        lax.psum(part_ln1_shift.astype(jnp.bfloat16), "band").astype(jnp.float32),
        lax.psum(part_ln2_gain.astype(jnp.bfloat16), "band").astype(jnp.float32),
        lax.psum(part_ln2_shift.astype(jnp.bfloat16), "band").astype(jnp.float32),
        lax.psum(part_w_up.astype(jnp.bfloat16), "band").astype(jnp.float32),
        lax.psum(part_b_up.astype(jnp.bfloat16), "band").astype(jnp.float32),
        lax.psum(part_w_down.astype(jnp.bfloat16), "band").astype(jnp.float32),
        lax.psum(part_b_down.astype(jnp.bfloat16), "band").astype(jnp.float32),
        lax.psum(part_scale_attn.astype(jnp.bfloat16), "band").astype(jnp.float32),
        lax.psum(part_scale_mlp.astype(jnp.bfloat16), "band").astype(jnp.float32),
    )
    return (
        output,
        input_grad,
        grad_w_qkv,
        grad_q_bias,
        grad_v_bias,
        grad_w_out,
        grad_b_out,
        grad_ln1_gain,
        grad_ln1_shift,
        grad_ln2_gain,
        grad_ln2_shift,
        grad_w_up,
        grad_b_up,
        grad_w_down,
        grad_b_down,
        grad_scale_attn,
        grad_scale_mlp,
    )


def solution(mesh):
    in_specs = (
        P("img", "band", None),
        P("img", "band", None),
        P("img"),
        P("img", None),
        P(),
        P(),
        P(),
        P(),
        P(),
        P(),
        P(),
        P(),
        P(),
        P(),
        P(),
        P(),
        P(),
        P(),
        P(),
    )
    out_specs = (
        P("img", "band", None),
        P("img", "band", None),
        P("img", None),
        P("img"),
        P("img"),
        P("img", None),
        P("img"),
        P("img"),
        P("img"),
        P("img"),
        P("img"),
        P("img", None),
        P("img"),
        P("img", None),
        P("img"),
        P("img"),
        P("img"),
    )
    return jax.shard_map(shards, mesh=mesh, in_specs=in_specs, out_specs=out_specs, check_vma=False)
```

profile of v0, /device:TPU:0, one launch (start us, length us, event | category | flops | bytes accessed | tf_op | source)
XLA Modules:
  0.0 930.3 jit_solution(7522192454892879542)
XLA Ops:
  10.2 3.3 fusion.62
  16.2 3.4 reshape.309
  19.6 2.4 copy.80
  22.0 4.3 all-to-all-start
  26.2 3.4 reshape.311
  29.7 2.4 copy.82
  32.0 9.3 %all-to-all-done = bf16[8,64,4,192]{3,1,0,2:T(8,128)(2,1)} async-done(((bf16[8,64,4,192]{3,1,0,2:T(8,128)(2,1)}), bf16[8,64,4,192]{3,1,0,2:T(8,128)(2,1)}, u32[]{:S(2)}, u32[]{:S(2)}) %all-to-all-start) | async-done | bytes 786464 | tf_op jit(solution)/shard_map/all_to_all | solution.py:134
  41.4 4.3 all-to-all-start.1
  45.6 2.4 slice.23
  48.0 3.4 reshape.313
  51.4 2.4 copy.84
  53.8 6.3 all-to-all-done.1
  60.1 4.7 all-to-all-start.2
  65.7 3.5 copy.81
  69.2 3.6 reshape.310
  72.8 3.5 copy.83
  76.2 3.6 reshape.312
  79.8 3.5 copy.85
  83.3 3.6 reshape.314
  87.9 30.6 %while.26 = (s32[]{:T(128)}, bf16[8,256,3,64]{1,3,2,0:T(8,128)(2,1)}, f32[8,3,256]{2,1,0:T(4,128)}, bf16[8,256,3,64]{1,3,2,0:T(8,128)(2,1)}, pred[8,256]{1,0:T(8...) while((s32[]{:T(128)}, ...), condition=%wide.region_5.6_spmd, body=%wide.region_2.5_spmd.sunk | while | flops 51952896 | bytes 2781029 | solution.py:139
  118.5 2.6 copy.86
  121.1 4.2 all-to-all-start.3
  126.0 13.8 %all-to-all-done.3 = bf16[8,256,1,192]{3,0,2,1:T(8,128)(2,1)} async-done(((bf16[8,256,1,192]{3,0,2,1:T(8,128)(2,1)}), bf16[8,256,1,192]{3,0,2,1:T(8,128)(2,1)}, u32[]{:S(2)}, u32[]{:S(2)}) %all-to-all-start.3) | async-done | bytes 786464 | tf_op jit(solution)/shard_map/all_to_all | solution.py:141
  143.1 3.0 reshape.316
  146.1 3.7 fusion.93
  150.2 6.9 fusion.80
  157.2 15.3 %multiply_convert_fusion.1 = (bf16[8,64,3072]{2,1,0:T(8,128)(2,1)}, f32[8,64,3072]{2,1,0:T(8,128)S(1)}) fusion(f32[8,64,3072]{2,1,0:T(8,128)S(1)} %get-tuple-element.203, f32[3072]{0:T(1024)S(1)} %copy-done.26, u8[64,3072]{1,0:T(8,128)(4,1)S(1)} %get-tuple-element.115, u8[64,3072]{1,0:T(8,128)(4,1)S(1)} %get-tuple-element.114), kind=kLoop, calls=%fused_computation.69 | loop fusion | flops 111673344 | bytes 16134144 | tf_op jit(solution)/shard_map/convert_element_type | solution.py:152
  172.5 9.4 %convert_reduce_fusion = (f32[3072]{0:T(1024)}, bf16[8,64,3072]{2,1,0:T(8,128)(2,1)}) fusion(f32[8,64,3072]{2,1,0:T(8,128)S(1)} %get-tuple-element.191, bf16[3072,768]{1,0:T(8,128)(2,1)} %param.38, bf16[8,64,768]{2,1,0:T(8,128)(2,1)} %param.24, f32[768]{0:T(1024)S(1)} %copy-done.35, f32[8,64]{1,0:T(8,128)S(1)} %copy-done.20, ...), kind=kOutput, calls=%fused_computation.67 | convolution fusion | flops 2444227584 | bytes 21263360 | tf_op jit(solution)/shard_map/nsd,fd->nsf/dot_general | solution.py:164
  181.9 6.9 multiply_reduce_fusion.3
  194.2 3.4 reshape.317
  197.6 2.4 copy.89
  200.0 4.2 all-to-all-start.4
  204.3 3.6 convolution_bitcast_fusion.3
  207.9 10.8 %all-to-all-done.4 = bf16[8,64,4,192]{3,1,0,2:T(8,128)(2,1)} async-done(((bf16[8,64,4,192]{3,1,0,2:T(8,128)(2,1)}), bf16[8,64,4,192]{3,1,0,2:T(8,128)(2,1)}, u32[]{:S(2)}, u32[]{:S(2)}) %all-to-all-start.4) | async-done | bytes 786464 | tf_op jit(solution)/shard_map/all_to_all | solution.py:186
  218.8 3.5 copy.90
  222.2 3.6 reshape.318
  228.8 70.4 %while.27 = (s32[]{:T(128)}, bf16[8,256,3,64]{1,3,2,0:T(8,128)(2,1)}, bf16[8,256,3,64]{1,3,2,0:T(8,128)(2,1)}, bf16[8,256,3,64]{1,3,2,0:T(8,128)(2,1)}, bf16[8,2...) while((s32[]{:T(128)}, ...), condition=%wide.region_12.13_spmd, body=%wide.region_10.12_spmd.sunk | while | flops 127843584 | bytes 6902653 | solution.py:188
  260.4 1.8 fusion.137
  299.1 2.6 copy.91
  301.7 4.3 all-to-all-start.5
  306.0 2.6 copy.94
  308.6 11.9 %all-to-all-done.5 = bf16[8,256,1,192]{3,0,2,1:T(8,128)(2,1)} async-done(((bf16[8,256,1,192]{3,0,2,1:T(8,128)(2,1)}), bf16[8,256,1,192]{3,0,2,1:T(8,128)(2,1)}, u32[]{:S(2)}, u32[]{:S(2)}) %all-to-all-start.5) | async-done | bytes 786464 | tf_op jit(solution)/shard_map/all_to_all | solution.py:192
  320.5 4.3 all-to-all-start.6
  324.8 2.6 copy.97
  327.4 11.9 %all-to-all-done.6 = bf16[8,256,1,192]{3,0,2,1:T(8,128)(2,1)} async-done(((bf16[8,256,1,192]{3,0,2,1:T(8,128)(2,1)}), bf16[8,256,1,192]{3,0,2,1:T(8,128)(2,1)}, u32[]{:S(2)}, u32[]{:S(2)}) %all-to-all-start.6) | async-done | bytes 786464 | tf_op jit(solution)/shard_map/all_to_all | solution.py:193
  339.3 4.3 all-to-all-start.7
  347.8 3.4 reshape.320
  354.4 3.0 reshape.322
  362.3 3.0 reshape.324
  369.2 5.2 convolution_bitcast_fusion.2
  375.1 9.0 convolution_bitcast_fusion.1
  384.8 8.5 convolution_bitcast_fusion
  400.0 4.7 fusion.90
  408.3 97.2 %reduce-scatter.5.cloned.1.call-done = f32[96,2304]{1,0:T(8,128)} async-done(((f32[768,2304]{1,0:T(8,128)}), f32[96,2304]{1,0:T(8,128)}) %reduce-scatter.5.cloned.1.call-update) | async-done | bytes 884752 | tf_op jit(solution)/shard_map/reduce_scatter | solution.py:226
  505.5 2.0 convert_element_type.201
  507.5 164.6 %reduce-scatter.9.cloned.1.call-done = f32[96,3072]{1,0:T(8,128)} async-done(((f32[768,3072]{1,0:T(8,128)}), f32[96,3072]{1,0:T(8,128)}) %reduce-scatter.9.cloned.1.call-update) | async-done | bytes 1179664 | tf_op jit(solution)/shard_map/reduce_scatter | solution.py:235
  672.1 2.2 convert_element_type.222
  674.3 164.2 %reduce-scatter.11.cloned.1.call-done = f32[384,768]{1,0:T(8,128)} async-done(((f32[3072,768]{1,0:T(8,128)}), f32[384,768]{1,0:T(8,128)}) %reduce-scatter.11.cloned.1.call-update) | async-done | bytes 1179664 | tf_op jit(solution)/shard_map/reduce_scatter | solution.py:237
  838.5 2.1 convert_element_type.227
  840.6 10.3 %multiply_reduce_fusion.1 = (f32[768]{0:T(1024)}, f32[768]{0:T(1024)}, f32[768]{0:T(1024)}, bf16[8,64,768]{2,1,0:T(8,128)(2,1)}, bf16[8,64,768]{2,1,0:T(8,128)(2,1)}) fusion(bf16[8,64,768]{2,1,0:T(8,128)(2,1)} %param.24, f32[768]{0:T(1024)} %param.39, f32[8,64]{1,0:T(8,128)S(1)} %copy-done.22, f32[8,64,768]{2,1,0:T(8,128)} %get-tuple-element.202, ...), kind=kOutput, calls=%fused_computation.121 | convolution fusion | flops 2426533632 | bytes 17332224 | tf_op jit(solution)/shard_map/nsf,fd->nsd/dot_general | solution.py:154
  851.0 36.7 %all-reduce.11 = (bf16[768]{0:T(1024)(128)(2,1)S(1)}, bf16[768]{0:T(1024)(128)(2,1)}, bf16[768]{0:T(1024)(128)(2,1)}, bf16[768]{0:T(1024)(128)(2,1)}, bf16[768]{...) all-reduce(f32[768]{0:T(1024)} %reduce_sum.234, ...), channel_id=3, replica_groups=mesh['img'=8,'band'=4] {'img'}, use_global_device_ids=true, to_apply=%region_18.19.clone | all-reduce | flops 10752 | bytes 64512
  897.9 6.5 all-reduce.12
  916.6 2.0 convert_element_type.202
  920.3 2.2 convert_element_type.223
  (259 shorter events, 170.7 us)
Async XLA Ops:
  7.2 3.0 copy-start
  10.2 3.3 copy-start.17
  10.2 3.3 copy-start.27
  10.2 3.3 copy-start.28
  13.6 2.6 copy-start.7
  22.0 19.4 %all-to-all-start = ((bf16[8,64,4,192]{3,1,0,2:T(8,128)(2,1)}), bf16[8,64,4,192]{3,1,0,2:T(8,128)(2,1)}, u32[]{:S(2)}, u32[]{:S(2)}) async-start(bf16[8,64,4,192]{3,1,0,2:T(8,128)(2,1)} %copy.80), calls=%async_computation | async-start | bytes 2097152 | tf_op jit(solution)/shard_map/all_to_all | solution.py:134
  41.4 18.8 %all-to-all-start.1 = ((bf16[8,64,4,192]{3,1,0,2:T(8,128)(2,1)}), bf16[8,64,4,192]{3,1,0,2:T(8,128)(2,1)}, u32[]{:S(2)}, u32[]{:S(2)}) async-start(bf16[8,64,4,192]{3,1,0,2:T(8,128)(2,1)} %copy.82), calls=%async_computation.1 | async-start | bytes 2097152 | tf_op jit(solution)/shard_map/all_to_all | solution.py:132
  51.4 13.5 %copy-start.32 = (s32[8]{0:T(128)S(1)}, s32[8]{0:T(128)}, u32[]{:S(2)}) copy-start(s32[8]{0:T(128)} %param.25) | copy-start | bytes 100
  60.1 19.7 %all-to-all-start.2 = ((bf16[8,64,4,192]{3,1,0,2:T(8,128)(2,1)}), bf16[8,64,4,192]{3,1,0,2:T(8,128)(2,1)}, u32[]{:S(2)}, u32[]{:S(2)}) async-start(bf16[8,64,4,192]{3,1,0,2:T(8,128)(2,1)} %copy.84), calls=%async_computation.2 | async-start | bytes 2097152 | tf_op jit(solution)/shard_map/all_to_all | solution.py:133
  121.1 18.8 %all-to-all-start.3 = ((bf16[8,256,1,192]{3,0,2,1:T(8,128)(2,1)}), bf16[8,256,1,192]{3,0,2,1:T(8,128)(2,1)}, u32[]{:S(2)}, u32[]{:S(2)}) async-start(bf16[8,256,1,192]{3,0,2,1:T(8,128)(2,1)} %copy.86), calls=%async_computation.3 | async-start | bytes 2097152 | tf_op jit(solution)/shard_map/all_to_all | solution.py:141
  141.3 4.8 copy-start.15
  146.1 4.1 copy-start.26
  146.1 4.1 copy-start.31
  146.1 4.1 copy-start.34
  149.8 38.9 %copy-start.1 = (f32[8,64,768]{2,1,0:T(8,128)}, f32[8,64,768]{2,1,0:T(8,128)S(1)}, u32[]{:S(2)}) copy-start(f32[8,64,768]{2,1,0:T(8,128)S(1)} %get-tuple-element.193) | copy-start | bytes 4718596
  150.2 38.6 %copy-start.24 = (f32[8,64]{1,0:T(8,128)}, f32[8,64]{1,0:T(8,128)S(1)}, u32[]{:S(2)}) copy-start(f32[8,64]{1,0:T(8,128)S(1)} %fusion.87) | copy-start | bytes 6148
  157.2 15.3 %copy-start.20 = (f32[8,64]{1,0:T(8,128)S(1)}, f32[8,64]{1,0:T(8,128)}, u32[]{:S(2)}) copy-start(f32[8,64]{1,0:T(8,128)} %and_convert_fusion.2) | copy-start | bytes 6148
  157.2 15.3 %copy-start.35 = (f32[768]{0:T(1024)S(1)}, f32[768]{0:T(1024)}, u32[]{:S(2)}) copy-start(f32[768]{0:T(1024)} %param.41) | copy-start | bytes 9220
  188.8 1.8 copy-start.11
  188.8 1.8 copy-start.16
  189.4 1.2 copy-start.6
  189.4 3.1 copy-start.10
  189.4 2.2 copy-start.23
  191.6 0.9 copy-start.12
  200.0 18.8 %all-to-all-start.4 = ((bf16[8,64,4,192]{3,1,0,2:T(8,128)(2,1)}), bf16[8,64,4,192]{3,1,0,2:T(8,128)(2,1)}, u32[]{:S(2)}, u32[]{:S(2)}) async-start(bf16[8,64,4,192]{3,1,0,2:T(8,128)(2,1)} %copy.89), calls=%async_computation.4 | async-start | bytes 2097152 | tf_op jit(solution)/shard_map/all_to_all | solution.py:186
  204.2 202.4 %reduce-scatter.7.cloned.1.call-start = ((), (), s32[]{:S(2)}) async-start(), calls=%async_computation.13 | async-start | bytes 2654208 | tf_op jit(solution)/shard_map/reduce_scatter | solution.py:229
  301.7 18.8 %all-to-all-start.5 = ((bf16[8,256,1,192]{3,0,2,1:T(8,128)(2,1)}), bf16[8,256,1,192]{3,0,2,1:T(8,128)(2,1)}, u32[]{:S(2)}, u32[]{:S(2)}) async-start(bf16[8,256,1,192]{3,0,2,1:T(8,128)(2,1)} %copy.91), calls=%async_computation.5 | async-start | bytes 2097152 | tf_op jit(solution)/shard_map/all_to_all | solution.py:192
  320.5 18.8 %all-to-all-start.6 = ((bf16[8,256,1,192]{3,0,2,1:T(8,128)(2,1)}), bf16[8,256,1,192]{3,0,2,1:T(8,128)(2,1)}, u32[]{:S(2)}, u32[]{:S(2)}) async-start(bf16[8,256,1,192]{3,0,2,1:T(8,128)(2,1)} %copy.94), calls=%async_computation.6 | async-start | bytes 2097152 | tf_op jit(solution)/shard_map/all_to_all | solution.py:193
  339.3 18.8 %all-to-all-start.7 = ((bf16[8,256,1,192]{3,0,2,1:T(8,128)(2,1)}), bf16[8,256,1,192]{3,0,2,1:T(8,128)(2,1)}, u32[]{:S(2)}, u32[]{:S(2)}) async-start(bf16[8,256,1,192]{3,0,2,1:T(8,128)(2,1)} %copy.97), calls=%async_computation.7 | async-start | bytes 2097152 | tf_op jit(solution)/shard_map/all_to_all | solution.py:194
  343.6 161.9 %reduce-scatter.5.cloned.1.call-start = ((), (), s32[]{:S(2)}) async-start(), calls=%async_computation.12 | async-start | bytes 7962624 | tf_op jit(solution)/shard_map/reduce_scatter | solution.py:226
  345.0 1.0 copy-start.4
  359.5 1.0 copy-start.5
  365.3 2.5 copy-start.8
  365.3 4.0 copy-start.2
  365.3 4.0 copy-start.18
  365.3 4.0 copy-start.29
  365.3 4.0 copy-start.33
  367.9 1.4 copy-start.14
  374.4 0.7 copy-start.25
  374.4 297.7 %reduce-scatter.9.cloned.1.call-start = ((), (), s32[]{:S(2)}) async-start(), calls=%async_computation.14 | async-start | bytes 10616832 | tf_op jit(solution)/shard_map/reduce_scatter | solution.py:235
  384.1 0.7 copy-start.21
  384.1 0.7 copy-start.36
  384.1 454.3 %reduce-scatter.11.cloned.1.call-start = ((), (), s32[]{:S(2)}) async-start(), calls=%async_computation.15 | async-start | bytes 10616832 | tf_op jit(solution)/shard_map/reduce_scatter | solution.py:237
  393.3 0.7 copy-start.37
  393.3 523.3 %all-reduce.16.cloned.1.call-start = ((), (), s32[]{:S(2)}) async-start(), calls=%async_computation.16 | async-start | bytes 3538944 | tf_op jit(solution)/shard_map/psum | solution.py:259
  400.0 4.7 copy-start.3
  400.0 4.7 copy-start.19
  400.0 4.7 copy-start.30
  404.7 1.4 copy-start.9
  507.5 333.1 %copy-start.22 = (f32[8,64]{1,0:T(8,128)S(1)}, f32[8,64]{1,0:T(8,128)}, u32[]{:S(2)}) copy-start(f32[8,64]{1,0:T(8,128)} %and_convert_fusion.2) | copy-start | bytes 6148
  916.6 5.9 copy-start.13
Sparse Core Ops, SparseCore 0:
  208.6 71.7 reduce-scatter.6
  374.6 130.8 reduce-scatter.4
  509.5 162.5 reduce-scatter.8
  676.0 162.4 reduce-scatter.10
  842.2 45.7 all-reduce.15
where the time goes:
time: 941 us; the launch traced here: 930 us
  waiting for transfers between devices  491 us (52%)
  matrix products  161 us (17%)
  local copies, waits for them, and re-layouts  122 us (13%)
  other arithmetic  62 us (7%)
  blocking collectives  43.2 us (5%)
  starting transfers between devices  34.8 us (4%)
  between operations  15.8 us (2%)
    reduce_scatter x1, waiting for transfers between devices, shards(): lax.psum_scatter(grad_w_up, 'img', scatter_dimension=0, tiled=True)  165 us
    reduce_scatter x1, waiting for transfers between devices, shards(): lax.psum_scatter(grad_w_down, 'img', scatter_dimension=0, tiled=True)  164 us
    reduce_scatter x1, waiting for transfers between devices, shards(): lax.psum_scatter(grad_w_qkv, 'img', scatter_dimension=0, tiled=True)  97.2 us
    unnamed x1, blocking collectives  36.7 us
    reshape x8, local copies, waits for them, and re-layouts, split_groups(): return entry.reshape(images, band_rows, band_count, group_width)  23.2 us
    unnamed x90, local copies, waits for them, and re-layouts  21.3 us
    dot_general x16, matrix products, masked_scores(): jnp.einsum('qhe,khe->hqk', queries, key_rows, preferred_element_type=jnp....  21 us
  transfers between devices with their start and end apart: 13, of which 10 were waited for; matrix products, arithmetic and copies ran while one was open for 23% of the time, Pallas kernels for 0%

commit v1 on v0

v1 whole, which is shorter than its diff:
```python
import jax
import jax.numpy as jnp
from jax import lax
from jax.sharding import PartitionSpec as P

HEAD = 64
GRID = 16
NEG_BIG = -1e30
EPSILON = 1e-06
F32 = jnp.float32
BF16 = jnp.bfloat16


def swap(entry, axis, mask):
    size = lax.axis_size(axis)
    return lax.ppermute(entry, axis, [(i, i ^ mask) for i in range(size)])


def norm_parts(entry):
    center = entry - jnp.mean(entry, -1, keepdims=True)
    spread = jnp.mean(center * center, -1, keepdims=True)
    inverse = lax.rsqrt(spread + EPSILON)
    return center * inverse, inverse


def norm_back(grad, gain, xhat, inverse):
    scaled = grad * gain
    inner = scaled - jnp.mean(scaled, -1, keepdims=True)
    inner = inner - xhat * jnp.mean(scaled * xhat, -1, keepdims=True)
    return inner * inverse, jnp.sum(grad * xhat, 0), jnp.sum(grad, 0)


def dot(left, right, dims):
    return lax.dot_general(left, right, (dims, ((), ())), preferred_element_type=F32)


def local_layer(x, cot, valid, key_ok, params):
    (w_qkv, q_bias, v_bias, w_out, b_out, g1, c1, g2, c2, w_up, b_up, w_down, b_down, s_attn, s_mlp) = params
    rows, width = x.shape
    images, slots = key_ok.shape
    heads = width // HEAD
    inputs = x.astype(F32)
    xhat1, inv1 = norm_parts(inputs)
    normed = (xhat1 * g1 + c1).astype(BF16)
    proj = dot(normed, w_qkv, ((1,), (0,)))
    q = (proj[:, :width] + q_bias).astype(BF16)
    k = proj[:, width : 2 * width].astype(BF16)
    v = (proj[:, 2 * width :] + v_bias).astype(BF16)

    def split(entry):
        return entry.reshape(images, slots, heads, HEAD)

    q, k, v = split(q), split(k), split(v)
    scores = jnp.einsum("nqhe,nkhe->nhqk", q, k, preferred_element_type=F32) * HEAD**-0.5
    scores = jnp.where(key_ok[:, None, None, :], scores, NEG_BIG)
    probs = jax.nn.softmax(scores, axis=-1)
    weights = probs.astype(BF16)
    attended = jnp.einsum("nhqk,nkhe->nqhe", weights, v, preferred_element_type=F32)
    attended = attended.astype(BF16).reshape(rows, width)
    branch = dot(attended, w_out, ((1,), (0,))) + b_out
    middle = inputs + s_attn * branch
    xhat2, inv2 = norm_parts(middle)
    normed2 = (xhat2 * g2 + c2).astype(BF16)
    pre = dot(normed2, w_up, ((1,), (0,))) + b_up
    hidden, pull = jax.vjp(lambda e: jax.nn.gelu(e, approximate=False), pre)
    hidden = hidden.astype(BF16)
    top = valid * cot.astype(F32)
    g_mlp = (s_mlp * top).astype(BF16)
    d_down_t = (g_mlp, hidden)
    d_pre = pull(dot(g_mlp, w_down, ((1,), (1,))))[0].astype(BF16)
    d_up = (normed2, d_pre)
    branch_mlp = dot(hidden, w_down, ((1,), (0,))) + b_down
    out = (valid * (middle + s_mlp * branch_mlp)).astype(BF16)
    d_norm2 = dot(d_pre, w_up, ((1,), (1,)))
    back2, d_g2, d_c2 = norm_back(d_norm2, g2, xhat2, inv2)
    d_middle = top + back2
    d_branch = (s_attn * d_middle).astype(BF16)
    d_wout = (attended, d_branch)
    d_att = split(dot(d_branch, w_out, ((1,), (1,))).astype(BF16))
    d_weights = jnp.einsum("nqhe,nkhe->nhqk", d_att, v, preferred_element_type=F32)
    d_scores = probs * (d_weights - jnp.sum(probs * d_weights, -1, keepdims=True))
    d_scores = d_scores.astype(BF16)
    d_q = jnp.einsum("nhqk,nkhe->nqhe", d_scores, k, preferred_element_type=F32) * HEAD**-0.5
    d_k = jnp.einsum("nhqk,nqhe->nkhe", d_scores, q, preferred_element_type=F32) * HEAD**-0.5
    d_v = jnp.einsum("nhqk,nqhe->nkhe", weights, d_att, preferred_element_type=F32)
    d_proj = jnp.concatenate([e.astype(BF16).reshape(rows, width) for e in (d_q, d_k, d_v)], -1)
    d_qkv = (normed, d_proj)
    d_norm1 = dot(d_proj, w_qkv, ((1,), (1,)))
    back1, d_g1, d_c1 = norm_back(d_norm1, g1, xhat1, inv1)
    grad_in = (d_middle + back1).astype(BF16)

    def total(entry):
        return jnp.sum(entry.astype(F32), 0)

    small = (
        total(d_proj[:, :width]),
        total(d_proj[:, 2 * width :]),
        total(d_branch),
        d_g1,
        d_c1,
        d_g2,
        d_c2,
        total(d_pre),
        total(g_mlp),
        total(d_middle * branch),
        total(top * branch_mlp),
    )
    return out, grad_in, d_down_t, d_up, d_wout, d_qkv, small


def halve(entry, axis, bit):
    got = swap(entry[1], axis, 1 << bit)
    return (entry[0].astype(F32) + got.astype(F32)).astype(BF16)


def both(entry, axis, bit):
    return (entry.astype(F32) + swap(entry, axis, 1 << bit).astype(F32)).astype(BF16)


def join(entry, axis, bit, dim):
    got = swap(entry, axis, 1 << bit)
    high = (lax.axis_index(axis) >> bit) & 1
    first = jnp.where(high == 1, got, entry)
    second = jnp.where(high == 1, entry, got)
    return jnp.concatenate([first, second], dim)


def scatter(blocks, order):
    r, c = blocks.shape[1:]
    if order == "yzx":
        b = blocks.reshape(2, 2, 2, r, c)
        b = halve(jnp.moveaxis(b, 2, 0), "img", 0)
        b = halve(jnp.moveaxis(b, 1, 0), "img", 1)
        b = halve(b, "img", 2)
        return both(b, "band", 1)
    b = blocks.reshape(2, 2, 2, 2, r // 2, c)
    high = (lax.axis_index("band") >> 1) & 1
    mine = lax.dynamic_index_in_dim(b, high, 3, False)
    other = lax.dynamic_index_in_dim(b, 1 - high, 3, False)
    b = (mine.astype(F32) + swap(other, "band", 2).astype(F32)).astype(BF16)
    b = halve(jnp.moveaxis(b, 2, 0), "img", 0)
    b = halve(jnp.moveaxis(b, 1, 0), "img", 1)
    b = halve(b, "img", 2)
    return join(b, "band", 1, 0)


def reduce_fast(left, right, width_blocks, col_type, cut):
    me = lax.axis_index("img")
    core = lax.axis_index("band") & 1
    perm = jnp.arange(8) ^ me
    if col_type:
        half = left.shape[1] // 2
        keep_l = lax.dynamic_slice_in_dim(left, core * half, half, 1)
        send_l = lax.dynamic_slice_in_dim(left, (1 - core) * half, half, 1)

        def make(l):
            g = dot(l, right, ((0,), (0,))).astype(BF16)
            return g.reshape(half, 8, -1).transpose(1, 0, 2)[perm]

        send, keep = make(send_l), make(keep_l)
    else:
        half = right.shape[1] // 2
        keep_r = lax.dynamic_slice_in_dim(right, core * half, half, 1)
        send_r = lax.dynamic_slice_in_dim(right, (1 - core) * half, half, 1)

        def make(r):
            g = dot(left, r, ((0,), (0,))).astype(BF16)
            return g.reshape(8, -1, half)[perm]

        send, keep = make(send_r), make(keep_r)
    got = swap(send, "band", 1)
    blocks = (keep.astype(F32) + got.astype(F32)).astype(BF16)
    if cut:
        if col_type:
            parts = [scatter(blocks[:, :cut], "yzx"), scatter(blocks[:, cut:], "xyz")]
            mine = jnp.concatenate(parts, 0)
        else:
            parts = [scatter(blocks[:, :, :cut], "yzx"), scatter(blocks[:, :, cut:], "xyz")]
            mine = jnp.concatenate(parts, 1)
    else:
        mine = scatter(blocks, "yzx")
    whole = join(mine, "band", 0, 0 if col_type else 1).astype(F32)
    return whole.T if col_type else whole


def reduce_plain(left, right, scale=None):
    grad = dot(left, right, ((0,), (0,)))
    part = lax.psum_scatter(grad, "img", scatter_dimension=0, tiled=True)
    return lax.psum(part.astype(BF16), "band").astype(F32)


def shards(
    tokens, cotangent, grid_side, visible, w_qkv, q_bias, v_bias, w_out, b_out, ln1_gain, ln1_shift,
    ln2_gain, ln2_shift, w_up, b_up, w_down, b_down, scale_attn, scale_mlp,
):
    images, band_rows, width = tokens.shape
    bands = lax.axis_size("band")
    band = lax.axis_index("band")
    mine = images // bands
    slots = bands * band_rows

    def to_images(entry):
        parts = []
        for q in range(bands):
            piece = lax.dynamic_slice_in_dim(entry, mine * (band ^ q), mine, 0)
            parts.append(swap(piece, "band", q) if q else piece)
        return jnp.concatenate(parts, 1).reshape(mine * slots, width)

    def to_bands(entry):
        entry = entry.reshape(mine, bands, band_rows, width)
        result = jnp.zeros((images, band_rows, width), entry.dtype)
        for q in range(bands):
            piece = entry[:, q]
            if q:
                piece = swap(piece, "band", q)
            result = lax.dynamic_update_slice_in_dim(result, piece, mine * (band ^ q), 0)
        return result

    sides = lax.dynamic_slice_in_dim(grid_side, band * mine, mine, 0)
    seen = lax.dynamic_slice_in_dim(visible, band * mine, mine, 0)
    order = jnp.arange(bands, dtype=jnp.int32) ^ band
    index = (order[:, None] * band_rows + jnp.arange(band_rows, dtype=jnp.int32)[None, :]).reshape(-1)
    inside = (index[None, :] // GRID < sides[:, None]) & (index[None, :] % GRID < sides[:, None])
    seen = seen.reshape(mine, bands, band_rows)[:, order].reshape(mine, slots)
    key_ok = inside & (seen == 1)
    valid = inside.astype(F32).reshape(mine * slots, 1)
    params = (
        w_qkv, q_bias, v_bias, w_out, b_out, ln1_gain, ln1_shift, ln2_gain, ln2_shift, w_up, b_up, w_down, b_down,
        scale_attn, scale_mlp,
    )
    x = to_images(tokens)
    cot = to_images(cotangent)
    out, grad_in, d_down, d_up, d_wout, d_qkv, small = local_layer(x, cot, valid, key_ok, params)
    output = to_bands(out)
    input_grad = to_bands(grad_in)
    if lax.axis_size("img") == 8 and bands == 4:
        grad_w_down = reduce_fast(d_down[0], d_down[1], 8, True, 224)
        grad_w_up = reduce_fast(*d_up, 8, False, 7 * 128)
        grad_w_out = reduce_fast(*d_wout, 8, False, 0)
        grad_w_qkv = reduce_fast(*d_qkv, 8, False, 5 * 128)
    else:
        grad_w_down = reduce_plain(d_down[1], d_down[0])
        grad_w_up = reduce_plain(*d_up)
        grad_w_out = reduce_plain(*d_wout)
        grad_w_qkv = reduce_plain(*d_qkv)
    small = lax.psum(jnp.concatenate(small), ("img", "band"))
    img = lax.axis_index("img")
    shares = []
    at = 0
    for size in (width,) * 7 + (w_up.shape[1],) + (width,) * 3:
        part = size // lax.axis_size("img")
        shares.append(lax.dynamic_slice_in_dim(small, at + img * part, part, 0))
        at += size
    (s_qb, s_vb, s_bo, s_g1, s_c1, s_g2, s_c2, s_bu, s_bd, s_sa, s_sm) = shares
    return (
        output, input_grad, grad_w_qkv, s_qb, s_vb, grad_w_out, s_bo, s_g1, s_c1, s_g2, s_c2, grad_w_up, s_bu,
        grad_w_down, s_bd, s_sa, s_sm,
    )


def solution(mesh):
    cut = P("img", "band", None)
    in_specs = (cut, cut, P("img"), P("img", None)) + (P(),) * 15
    row, vec = P("img", None), P("img")
    out_specs = (cut, cut, row, vec, vec, row, vec, vec, vec, vec, vec, row, vec, row, vec, vec, vec)
    return jax.shard_map(shards, mesh=mesh, in_specs=in_specs, out_specs=out_specs, check_vma=False)
```

time: 941 us -> 424 us (0.45)
  waiting for transfers between devices: 491 us -> 94.5 us
  matrix products: 161 us -> 86.9 us
  other arithmetic: 62 us -> 43.8 us
  local copies, waits for them, and re-layouts: 122 us -> 105 us
  between operations: 15.8 us -> 2.69 us
    reduce_scatter x4 -> x0, waiting for transfers between devices: 426 us -> none  [the longest x1 165 us: shards(): lax.psum_scatter(grad_w_up, 'img', scatter_dimension=0, tiled=True)]
    ppermute x0 -> x51, waiting for transfers between devices: none -> 94.5 us  [swap(): return lax.ppermute(entry, axis, [(i, i ^ mask) for i in range(size)])]
    dot_general x68 -> x22, matrix products: 161 us -> 86.9 us  [the longest x16 67.9 us: dot(): lax.dot_general(left, right, (dims, ((), ())), preferred_element_type=F32)]
    all_to_all x8 -> x0, waiting for transfers between devices: 64.9 us -> none  [the longest x1 13.8 us: shards(): lax.all_to_all(join_groups(attended), 'band', split_axis=1, concat_axis=2...]
    ppermute x0 -> x51, starting transfers between devices: none -> 44.1 us  [swap(): return lax.ppermute(entry, axis, [(i, i ^ mask) for i in range(size)])]
    reshape x20 -> x8, local copies, waits for them, and re-layouts: 60.3 us -> 17.1 us  [the longest x4 11.9 us: split(): return entry.reshape(images, slots, heads, HEAD)]
    unnamed x1 -> x0, blocking collectives: 36.7 us -> none
    all_to_all x8 -> x0, starting transfers between devices: 34.5 us -> none  [the longest x1 4.71 us: shards(): lax.all_to_all(split_groups(key_rows), 'band', split_axis=2, concat_axis=...]
  transfers between devices with their start and end apart: 13 -> 51, of which waited for: 10 -> 25; matrix products, arithmetic and copies ran while one was open for 23% -> 34% of each run, Pallas kernels for 0% -> 0%
where the time goes in v1:
time: 424 us; the launch traced here: 418 us
  local copies, waits for them, and re-layouts  105 us (25%)
  waiting for transfers between devices  94.5 us (22%)
  matrix products  86.9 us (20%)
  starting transfers between devices  44.1 us (10%)
  other arithmetic  43.8 us (10%)
  blocking collectives  40.8 us (10%)
    ppermute x51, waiting for transfers between devices, swap(): return lax.ppermute(entry, axis, [(i, i ^ mask) for i in range(size)])  94.5 us
    dot_general x16, matrix products, dot(): lax.dot_general(left, right, (dims, ((), ())), preferred_element_type=F32)  67.9 us
    ppermute x51, starting transfers between devices, swap(): return lax.ppermute(entry, axis, [(i, i ^ mask) for i in range(size)])  44.1 us
    psum x1, blocking collectives, shards(): small = lax.psum(jnp.concatenate(small), ('img', 'band'))  40.8 us
    unnamed x162, local copies, waits for them, and re-layouts  25.7 us
    gather x6, local copies, waits for them, and re-layouts, make(): return g.reshape(8, -1, half)[perm]  20.2 us
    reshape x4, local copies, waits for them, and re-layouts, split(): return entry.reshape(images, slots, heads, HEAD)  11.9 us
  transfers between devices with their start and end apart: 51, of which 25 were waited for; matrix products, arithmetic and copies ran while one was open for 34% of the time, Pallas kernels for 0%

profile of v1, /device:TPU:0, one launch (start us, length us, event | category | flops | bytes accessed | tf_op | source)
XLA Modules:
  0.0 417.9 jit_solution(14339565552253459809)
XLA Ops:
  0.7 2.3 constant_dynamic-slice_fusion.14
  3.4 2.5 collective-permute-start.1
  6.1 2.1 constant_dynamic-slice_fusion.9
  26.5 2.3 copy.104
  28.7 3.1 reshape.478
  31.8 2.3 copy.105
  34.1 2.9 reshape.479
  37.0 2.3 copy.101
  39.3 2.9 reshape.476
  42.2 2.4 fusion.62
  44.6 2.7 fusion.117
  51.4 2.3 fusion.115
  54.5 2.6 fusion.119
  58.6 20.0 %convert_reduce_fusion = (f32[3072]{0:T(1024)}, bf16[512,3072]{1,0:T(8,128)(2,1)}, f32[512,3072]{1,0:T(8,128)}) fusion(f32[512,3072]{1,0:T(8,128)S(1)} %fusion.119, f32[3072]{0:T(1024)S(1)} %copy-done.48, bf16[512,768]{1,0:T(8,128)(2,1)S(1)} %multiply_convert_fusion.6, bf16[3072,768]{1,0:T(8,128)(2,1)S(1)} %bitcast.450), kind=kOutput, calls=%fused_computation.12 | convolution fusion | flops 2533880832 | bytes 21258240 | tf_op jit(solution)/shard_map/dot_general | solution.py:34
  78.6 4.3 %multiply_convert_fusion.1 = bf16[512,3072]{1,0:T(8,128)(2,1)S(1)} fusion(f32[512,3072]{1,0:T(8,128)} %get-tuple-element.65, f32[512,3072]{1,0:T(8,128)S(1)} %fusion.119, f32[3072]{0:T(1024)S(1)} %copy-done.48), kind=kLoop, calls=%fused_computation.16 | loop fusion | flops 6291456 | bytes 15740928 | tf_op jit(solution)/shard_map/convert_element_type | solution.py:66
  82.8 2.9 convolution_convert_fusion
  85.8 2.9 convolution_convert_fusion.1
  88.7 5.1 %fusion.120 = f32[512,768]{1,0:T(8,128)S(1)} fusion(bf16[512,3072]{1,0:T(8,128)(2,1)S(1)} %copy-done.62, bf16[768,3072]{1,0:T(8,128)(2,1)} %param.32), kind=kOutput, calls=%fused_computation.347 | convolution fusion | flops 2415919104 | bytes 9437184 | tf_op jit(solution)/shard_map/dot_general | solution.py:34
  93.8 5.6 %multiply_reduce_fusion.1 = (f32[768]{0:T(1024)}, bf16[512,768]{1,0:T(8,128)(2,1)}, f32[768]{0:T(1024)}, f32[512]{0:T(512)S(1)}, f32[512]{0:T(512)S(1)}, /*index=5*/f32[768]{0:T(1024)}) fusion(f32[768]{0:T(1024)S(1)} %copy-done.60, f32[512]{0:T(512)S(1)} %bitcast.447, bf16[2,64,768]{2,1,0:T(8,128)(2,1)} %collective-permute-done.8, ...), kind=kOutput, calls=%fused_computation.75 | convolution fusion | flops 2425746176 | bytes 12611584 | tf_op jit(solution)/shard_map/dot_general | solution.py:34
  106.8 2.4 copy.115
  109.1 3.1 reshape.482
  112.2 5.7 %convert_reduce_fusion.4 = (f32[12,64]{1,0:T(8,128)}, bf16[2,256,12,64]{1,3,2,0:T(8,128)(2,1)}) fusion(f32[2,12,256,256]{2,3,1,0:T(8,128)} %copy-done.11, f32[2,12,256]{2,1,0:T(8,128)} %copy-done.35, bf16[2,256,12,64]{1,0,3,2:T(2,128)(2,1)} %reshape.482), kind=kOutput, calls=%fused_computation.81 | convolution fusion | flops 205651200 | bytes 7891968 | tf_op jit(solution)/shard_map/nhqk,nqhe->nkhe/dot_general | solution.py:85
  118.0 6.8 %multiply_reduce_fusion = (f32[2,12,256]{2,1,0:T(8,128)S(1)}, f32[2,12,256,256]{2,3,1,0:T(8,128)}) fusion(f32[2,12,256,256]{2,3,1,0:T(8,128)} %copy-done.11, f32[2,12,256]{2,1,0:T(8,128)S(1)} %copy-done.36, bf16[2,256,12,64]{1,0,3,2:T(2,128)(2,1)S(1)} %copy-done.25, bf16[2,256,12,64]{1,0,3,2:T(2,128)(2,1)S(1)} %copy-done.26), kind=kOutput, calls=%fused_computation.14 | convolution fusion | flops 206039040 | bytes 14204928 | tf_op jit(solution)/shard_map/nqhe,nkhe->nhqk/dot_general | solution.py:80
  124.8 4.3 %multiply_convert_fusion = bf16[2,12,256,256]{2,3,1,0:T(8,128)(2,1)S(1)} fusion(f32[2,12,256,256]{2,3,1,0:T(8,128)} %get-tuple-element.132, f32[2,12,256]{2,1,0:T(8,128)S(1)} %get-tuple-element.131, f32[2,12,256,256]{2,3,1,0:T(8,128)S(1)} %bitcast.408, f32[2,12,256]{2,1,0:T(8,128)S(1)} %copy-done.36), kind=kLoop, calls=%fused_computation.13 | loop fusion | flops 6291456 | bytes 15777792 | tf_op jit(solution)/shard_map/convert_element_type | solution.py:82
  134.3 4.1 gather_fusion.8
  138.6 3.4 copy.219
  142.0 4.2 gather_fusion.7
  146.1 4.5 %convolution_convert_fusion.2 = bf16[768,1536]{1,0:T(8,128)(2,1)} fusion(bf16[512,768]{1,0:T(8,128)(2,1)} %copy-done.16, bf16[512,3072]{1,0:T(8,128)(2,1)} %get-tuple-element.64, s32[]{:T(128)S(6)} %select_n.262), kind=kOutput, calls=%fused_computation.38 | convolution fusion | flops 1209139200 | bytes 4718596 | tf_op jit(solution)/shard_map/dot_general | solution.py:34
  150.7 3.9 gather_fusion.6
  154.9 4.5 %convolution_convert_fusion.3 = bf16[768,1536]{1,0:T(8,128)(2,1)} fusion(bf16[512,768]{1,0:T(8,128)(2,1)} %copy-done.16, bf16[512,3072]{1,0:T(8,128)(2,1)} %get-tuple-element.64, s32[]{:T(128)S(6)} %select_n.261), kind=kOutput, calls=%fused_computation.39 | convolution fusion | flops 1209139200 | bytes 4718596 | tf_op jit(solution)/shard_map/dot_general | solution.py:34
  159.4 3.9 gather_fusion.5
  163.2 2.6 gather_fusion.4
  166.1 2.6 gather_fusion.3
  176.3 2.5 convolution_convert_fusion.4
  178.8 3.6 gather_fusion.2
  182.3 4.0 convolution_convert_fusion.5
  186.3 3.6 gather_fusion.1
  189.9 4.5 %fusion.27 = (f32[768]{0:T(1024)S(1)}, f32[512]{0:T(512)S(1)}, f32[512]{0:T(512)S(1)}, f32[768]{0:T(1024)S(1)}, f32[512,768]{1,0:T(8,128)S(1)}) fusion(f32[512]{0:T(512)S(1)} %bitcast.441, f32[512]{0:T(512)S(1)} %bitcast.444, bf16[2,64,768]{2,1,0:T(8,128)(2,1)} %collective-permute-done.2, bf16[2,64,768]{2,1,0:T(8,128)(2,1)} %collective-permute-done.1, ...), kind=kOutput, calls=%fused_computation.72 | convolution fusion | flops 1818621440 | bytes 8274944 | tf_op jit(solution)/shard_map/dot_general | solution.py:34
  215.6 40.8 %psum.7 = f32[10752]{0:T(1024)} all-reduce(f32[10752]{0:T(1024)} %constant_dynamic-update-slice_fusion.12), channel_id=1, replica_groups=mesh['img'=8,'band'=4] {'img','band'}, use_global_device_ids=true, to_apply=%region_22.23 | all-reduce | flops 10752 | bytes 86016 | tf_op jit(solution)/shard_map/psum | solution.py:246
  261.5 2.3 collective-permute-start.24
  270.2 2.8 collective-permute-done.11
  276.2 3.0 collective-permute-done.25
  282.9 4.9 %collective-permute-done.26 = bf16[96,384]{1,0:T(8,128)(2,1)S(1)} collective-permute-done((bf16[96,384]{1,0:T(8,128)(2,1)S(1)}, bf16[96,384]{1,0:T(8,128)(2,1)S(1)}, u32[]{:S(2)}, u32[]{:S(2)}) %collective-permute-start.26) | collective-permute-done | bytes 73760 | tf_op jit(solution)/shard_map/ppermute | solution.py:16
  289.2 3.0 collective-permute-done.27
  295.9 8.7 %collective-permute-done.17 = bf16[2,2,2,48,512]{4,3,0,1,2:T(8,128)(2,1)S(1)} collective-permute-done((bf16[2,2,2,48,512]{4,3,0,1,2:T(8,128)(2,1)S(1)}, bf16[2,2,2,48,512]{4,3,0,1,2:T(8,128)(2,1)S(1)}, u32[]{:S(2)}, u32[]{:S(2)}) %collective-permute-start.17) | collective-permute-done | bytes 393248 | tf_op jit(solution)/shard_map/ppermute | solution.py:16
  305.3 3.4 collective-permute-done.13
  309.0 2.2 add_convert_fusion.1
  311.4 2.3 copy-done.4
  313.8 2.3 add_convert_fusion.2
  322.5 2.5 collective-permute-done.19
  326.9 2.9 collective-permute-start.20
  329.9 4.3 %collective-permute-done.20 = bf16[48,512]{1,0:T(8,128)(2,1)S(1)} collective-permute-done((bf16[48,512]{1,0:T(8,128)(2,1)S(1)}, bf16[48,512]{1,0:T(8,128)(2,1)S(1)}, u32[]{:S(2)}, u32[]{:S(2)}) %collective-permute-start.20) | collective-permute-done | bytes 49184 | tf_op jit(solution)/shard_map/ppermute | solution.py:16
  335.4 5.6 %collective-permute-done.15 = bf16[96,640]{1,0:T(8,128)(2,1)S(1)} collective-permute-done((bf16[96,640]{1,0:T(8,128)(2,1)S(1)}, bf16[96,640]{1,0:T(8,128)(2,1)S(1)}, u32[]{:S(2)}, u32[]{:S(2)}) %collective-permute-start.15) | collective-permute-done | bytes 122912 | tf_op jit(solution)/shard_map/ppermute | solution.py:16
  341.1 4.1 collective-permute-done.21
  345.1 4.9 %collective-permute-done.16 = bf16[96,640]{1,0:T(8,128)(2,1)S(1)} collective-permute-done((bf16[96,640]{1,0:T(8,128)(2,1)S(1)}, bf16[96,640]{1,0:T(8,128)(2,1)S(1)}, u32[]{:S(2)}, u32[]{:S(2)}) %collective-permute-start.16) | collective-permute-done | bytes 122912 | tf_op jit(solution)/shard_map/ppermute | solution.py:16
  356.3 2.8 collective-permute-done.46
  359.3 4.7 %collective-permute-done.35 = bf16[2,2,48,640]{3,2,0,1:T(8,128)(2,1)S(1)} collective-permute-done((bf16[2,2,48,640]{3,2,0,1:T(8,128)(2,1)S(1)}, bf16[2,2,48,640]{3,2,0,1:T(8,128)(2,1)S(1)}, u32[]{:S(2)}, u32[]{:S(2)}) %collective-permute-start.35) | collective-permute-done | bytes 245792 | tf_op jit(solution)/shard_map/ppermute | solution.py:16
  364.2 10.8 %collective-permute-done.47 = bf16[2,80,384]{2,1,0:T(8,128)(2,1)S(1)} collective-permute-done((bf16[2,80,384]{2,1,0:T(8,128)(2,1)S(1)}, bf16[2,80,384]{2,1,0:T(8,128)(2,1)S(1)}, u32[]{:S(2)}, u32[]{:S(2)}) %collective-permute-start.47) | collective-permute-done | bytes 122912 | tf_op jit(solution)/shard_map/ppermute | solution.py:16
  378.3 3.3 collective-permute-done.48
  383.8 2.1 collective-permute-done.49
  388.1 2.4 collective-permute-start.32
  390.5 10.3 %collective-permute-done.43 = bf16[224,384]{1,0:T(8,128)(2,1)S(1)} collective-permute-done((bf16[224,384]{1,0:T(8,128)(2,1)S(1)}, bf16[224,384]{1,0:T(8,128)(2,1)S(1)}, u32[]{:S(2)}, u32[]{:S(2)}) %collective-permute-start.43) | collective-permute-done | bytes 172064 | tf_op jit(solution)/shard_map/ppermute | solution.py:16
  404.1 3.7 collective-permute-done.44
  412.7 2.7 copy.147
  (391 shorter events, 124.7 us)
Async XLA Ops:
  0.7 21.3 %copy-start = (bf16[768,2304]{1,0:T(8,128)(2,1)S(1)}, bf16[768,2304]{1,0:T(8,128)(2,1)}, u32[]{:S(2)}) copy-start(bf16[768,2304]{1,0:T(8,128)(2,1)} %param.23) | copy-start | bytes 10616836
  0.7 19.7 %copy-start.46 = (f32[768]{0:T(1024)S(1)}, f32[768]{0:T(1024)}, u32[]{:S(2)}) copy-start(f32[768]{0:T(1024)} %param.28) | copy-start | bytes 9220
  3.0 13.7 %collective-permute-start = (bf16[2,64,768]{2,1,0:T(8,128)(2,1)}, bf16[2,64,768]{2,1,0:T(8,128)(2,1)}, u32[]{:S(2)}, u32[]{:S(2)}) collective-permute-start(bf16[2,64,768]{2,1,0:T(8,128)(2,1)} %get-tuple-element.95), channel_id=1, source_target_pairs={{0,1},{1,0},{2,3},{3,2},{4,5},{5,4},{6,7},{7,6},{8,9},{9,8},{10,11... | collective-permute-start | bytes 589832 | tf_op jit(solution)/shard_map/ppermute | solution.py:16
  3.4 13.3 %collective-permute-start.1 = (bf16[2,64,768]{2,1,0:T(8,128)(2,1)}, bf16[2,64,768]{2,1,0:T(8,128)(2,1)}, u32[]{:S(2)}, u32[]{:S(2)}) collective-permute-start(bf16[2,64,768]{2,1,0:T(8,128)(2,1)} %get-tuple-element.97), channel_id=1, source_target_pairs={{0,2},{1,3},{2,0},{3,1},{4,6},{5,7},{6,4},{7,5},{8,10},{9,11},{10,... | collective-permute-start | bytes 589832 | tf_op jit(solution)/shard_map/ppermute | solution.py:16
  5.9 10.8 %collective-permute-start.2 = (bf16[2,64,768]{2,1,0:T(8,128)(2,1)}, bf16[2,64,768]{2,1,0:T(8,128)(2,1)}, u32[]{:S(2)}, u32[]{:S(2)}) collective-permute-start(bf16[2,64,768]{2,1,0:T(8,128)(2,1)} %get-tuple-element.96), channel_id=1, source_target_pairs={{0,3},{1,2},{2,1},{3,0},{4,7},{5,6},{6,5},{7,4},{8,11},{9,10},{10,... | collective-permute-start | bytes 589832 | tf_op jit(solution)/shard_map/ppermute | solution.py:16
  8.2 49.0 %collective-permute-start.6 = (bf16[2,64,768]{2,1,0:T(8,128)(2,1)}, bf16[2,64,768]{2,1,0:T(8,128)(2,1)}, u32[]{:S(2)}, u32[]{:S(2)}) collective-permute-start(bf16[2,64,768]{2,1,0:T(8,128)(2,1)} %get-tuple-element.91), channel_id=1, source_target_pairs={{0,1},{1,0},{2,3},{3,2},{4,5},{5,4},{6,7},{7,6},{8,9},{9,8},{10,11... | collective-permute-start | bytes 589832 | tf_op jit(solution)/shard_map/ppermute | solution.py:16
  8.3 48.9 %collective-permute-start.7 = (bf16[2,64,768]{2,1,0:T(8,128)(2,1)}, bf16[2,64,768]{2,1,0:T(8,128)(2,1)}, u32[]{:S(2)}, u32[]{:S(2)}) collective-permute-start(bf16[2,64,768]{2,1,0:T(8,128)(2,1)} %get-tuple-element.93), channel_id=1, source_target_pairs={{0,2},{1,3},{2,0},{3,1},{4,6},{5,7},{6,4},{7,5},{8,10},{9,11},{10,... | collective-permute-start | bytes 589832 | tf_op jit(solution)/shard_map/ppermute | solution.py:16
  16.7 40.5 %collective-permute-start.8 = (bf16[2,64,768]{2,1,0:T(8,128)(2,1)}, bf16[2,64,768]{2,1,0:T(8,128)(2,1)}, u32[]{:S(2)}, u32[]{:S(2)}) collective-permute-start(bf16[2,64,768]{2,1,0:T(8,128)(2,1)} %get-tuple-element.92), channel_id=1, source_target_pairs={{0,3},{1,2},{2,1},{3,0},{4,7},{5,6},{6,5},{7,4},{8,11},{9,10},{10,... | collective-permute-start | bytes 589832 | tf_op jit(solution)/shard_map/ppermute | solution.py:16
  112.2 12.6 %slice-start.2 = ((s8[6291456]{0:T(1024)(128)(4,1)}), s8[4194304]{0:T(1024)(128)(4,1)S(1)}, s32[]{:S(2)}) async-start(s8[6291456]{0:T(1024)(128)(4,1)} %bitcast.407), calls=%async_computation.2 | async-start | bytes 8388608
  138.4 170.6 %collective-permute-start.40 = (bf16[8,384,384]{2,1,0:T(8,128)(2,1)}, bf16[8,384,384]{2,1,0:T(8,128)(2,1)}, u32[]{:S(2)}, u32[]{:S(2)}) collective-permute-start(bf16[8,384,384]{2,1,0:T(8,128)(2,1)} %gather_fusion.8), channel_id=1, source_target_pairs={{0,1},{1,0},{2,3},{3,2},{4,5},{5,4},{6,7},{7,6},{8,9},{9,8},{10,11... | collective-permute-start | bytes 7077896 | tf_op jit(solution)/shard_map/ppermute | solution.py:16
  154.6 156.8 %collective-permute-start.29 = (bf16[8,96,1536]{2,1,0:T(8,128)(2,1)}, bf16[8,96,1536]{2,1,0:T(8,128)(2,1)}, u32[]{:S(2)}, u32[]{:S(2)}) collective-permute-start(bf16[8,96,1536]{2,1,0:T(8,128)(2,1)} %gather_fusion.6), channel_id=1, source_target_pairs={{0,1},{1,0},{2,3},{3,2},{4,5},{5,4},{6,7},{7,6},{8,9},{9,8},{10,11... | collective-permute-start | bytes 7077896 | tf_op jit(solution)/shard_map/ppermute | solution.py:16
  165.9 94.3 %collective-permute-start.23 = (bf16[8,96,384]{2,1,0:T(8,128)(2,1)}, bf16[8,96,384]{2,1,0:T(8,128)(2,1)}, u32[]{:S(2)}, u32[]{:S(2)}) collective-permute-start(bf16[8,96,384]{2,1,0:T(8,128)(2,1)} %gather_fusion.4), channel_id=1, source_target_pairs={{0,1},{1,0},{2,3},{3,2},{4,5},{5,4},{6,7},{7,6},{8,9},{9,8},{10,11... | collective-permute-start | bytes 1769480 | tf_op jit(solution)/shard_map/ppermute | solution.py:16
  196.2 11.5 %copy-start.56 = (f32[768]{0:T(1024)S(1)}, f32[768]{0:T(1024)}, u32[]{:S(2)}) copy-start(f32[768]{0:T(1024)} %get-tuple-element.74) | copy-start | bytes 9220
  196.2 12.8 %copy-start.49 = (f32[3072]{0:T(1024)S(1)}, f32[3072]{0:T(1024)}, u32[]{:S(2)}) copy-start(f32[3072]{0:T(1024)} %get-tuple-element.63) | copy-start | bytes 36868
  196.2 14.1 %copy-start.18 = (bf16[2,64,768]{2,1,0:T(8,128)(2,1)S(1)}, bf16[2,64,768]{2,1,0:T(8,128)(2,1)}, u32[]{:S(2)}) copy-start(bf16[2,64,768]{2,1,0:T(8,128)(2,1)} %get-tuple-element.90) | copy-start | bytes 589828
  196.2 14.1 %copy-start.50 = (f32[2,256]{1,0:T(2,128)S(1)}, f32[2,256]{1,0:T(2,128)}, u32[]{:S(2)}) copy-start(f32[2,256]{1,0:T(2,128)} %get-tuple-element.61) | copy-start | bytes 6148
  196.2 18.1 %copy-start.55 = (f32[768]{0:T(1024)S(1)}, f32[768]{0:T(1024)}, u32[]{:S(2)}) copy-start(f32[768]{0:T(1024)} %get-tuple-element.72) | copy-start | bytes 9220
  197.1 68.2 %collective-permute-start.9 = (bf16[2,64,768]{2,1,0:T(8,128)(2,1)}, bf16[2,64,768]{2,1,0:T(8,128)(2,1)}, u32[]{:S(2)}, u32[]{:S(2)}) collective-permute-start(bf16[2,64,768]{2,1,0:T(8,128)(2,1)} %get-tuple-element.86), channel_id=1, source_target_pairs={{0,1},{1,0},{2,3},{3,2},{4,5},{5,4},{6,7},{7,6},{8,9},{9,8},{10,11... | collective-permute-start | bytes 589832 | tf_op jit(solution)/shard_map/ppermute | solution.py:16
  198.3 68.0 %collective-permute-start.10 = (bf16[2,64,768]{2,1,0:T(8,128)(2,1)}, bf16[2,64,768]{2,1,0:T(8,128)(2,1)}, u32[]{:S(2)}, u32[]{:S(2)}) collective-permute-start(bf16[2,64,768]{2,1,0:T(8,128)(2,1)} %get-tuple-element.85), channel_id=1, source_target_pairs={{0,2},{1,3},{2,0},{3,1},{4,6},{5,7},{6,4},{7,5},{8,10},{9,11},{10,... | collective-permute-start | bytes 589832 | tf_op jit(solution)/shard_map/ppermute | solution.py:16
  261.5 30.9 %copy-start.8 = (bf16[8,96,1152]{2,1,0:T(8,128)(2,1)S(1)}, bf16[8,96,1152]{2,1,0:T(8,128)(2,1)}, u32[]{:S(2)}) copy-start(bf16[8,96,1152]{2,1,0:T(8,128)(2,1)} %gather_fusion.1) | copy-start | bytes 5308420
  261.5 8.6 %collective-permute-start.24 = (bf16[2,2,96,384]{3,2,1,0:T(8,128)(2,1)S(1)}, bf16[2,2,96,384]{3,2,1,0:T(8,128)(2,1)S(1)}, u32[]{:S(2)}, u32[]{:S(2)}) collective-permute-start(bf16[2,2,96,384]{3,2,1,0:T(8,128)(2,1)S(1)} %slice_bitcast_fusion.10), channel_id=1, source_target_pairs={{0,4},{4,0},{8,12},{12,8},{16,20},{20,16},{24,28},{28,24},{1,5},{5... | collective-permute-start | bytes 884744 | tf_op jit(solution)/shard_map/ppermute | solution.py:16
  265.3 27.0 %collective-permute-start.12 = (bf16[8,96,1152]{2,1,0:T(8,128)(2,1)S(1)}, bf16[8,96,1152]{2,1,0:T(8,128)(2,1)S(1)}, u32[]{:S(2)}, u32[]{:S(2)}) collective-permute-start(bf16[8,96,1152]{2,1,0:T(8,128)(2,1)S(1)} %copy-done.20), channel_id=1, source_target_pairs={{0,1},{1,0},{2,3},{3,2},{4,5},{5,4},{6,7},{7,6},{8,9},{9,8},{10,11... | collective-permute-start | bytes 5308424 | tf_op jit(solution)/shard_map/ppermute | solution.py:16
  266.4 6.7 %collective-permute-start.11 = (bf16[2,64,768]{2,1,0:T(8,128)(2,1)S(1)}, bf16[2,64,768]{2,1,0:T(8,128)(2,1)S(1)}, u32[]{:S(2)}, u32[]{:S(2)}) collective-permute-start(bf16[2,64,768]{2,1,0:T(8,128)(2,1)S(1)} %copy-done.34), channel_id=1, source_target_pairs={{0,3},{1,2},{2,1},{3,0},{4,7},{5,6},{6,5},{7,4},{8,11},{9,10},{10,... | collective-permute-start | bytes 589832 | tf_op jit(solution)/shard_map/ppermute | solution.py:16
  270.1 4.5 %collective-permute-start.3 = (bf16[2,64,768]{2,1,0:T(8,128)(2,1)S(1)}, bf16[2,64,768]{2,1,0:T(8,128)(2,1)S(1)}, u32[]{:S(2)}, u32[]{:S(2)}) collective-permute-start(bf16[2,64,768]{2,1,0:T(8,128)(2,1)S(1)} %get-tuple-element.89), channel_id=1, source_target_pairs={{0,1},{1,0},{2,3},{3,2},{4,5},{5,4},{6,7},{7,6},{8,9},{9,8},{10,11... | collective-permute-start | bytes 589832 | tf_op jit(solution)/shard_map/ppermute | solution.py:16
  273.0 6.2 %collective-permute-start.25 = (bf16[2,96,384]{2,1,0:T(8,128)(2,1)S(1)}, bf16[2,96,384]{2,1,0:T(8,128)(2,1)S(1)}, u32[]{:S(2)}, u32[]{:S(2)}) collective-permute-start(bf16[2,96,384]{2,1,0:T(8,128)(2,1)S(1)} %slice_bitcast_fusion.32), channel_id=1, source_target_pairs={{0,8},{4,12},{8,0},{12,4},{16,24},{20,28},{24,16},{28,20},{1,9},{5... | collective-permute-start | bytes 442376 | tf_op jit(solution)/shard_map/ppermute | solution.py:16
  274.5 17.8 %copy-start.30 = (bf16[8,64,768]{2,1,0:T(8,128)(2,1)}, bf16[8,64,768]{2,1,0:T(8,128)(2,1)S(1)}, u32[]{:S(2)}) copy-start(bf16[8,64,768]{2,1,0:T(8,128)(2,1)S(1)} %constant_dynamic-update-slice_fusion.4) | copy-start | bytes 2359300
  274.6 7.0 %collective-permute-start.4 = (bf16[2,64,768]{2,1,0:T(8,128)(2,1)S(1)}, bf16[2,64,768]{2,1,0:T(8,128)(2,1)S(1)}, u32[]{:S(2)}, u32[]{:S(2)}) collective-permute-start(bf16[2,64,768]{2,1,0:T(8,128)(2,1)S(1)} %get-tuple-element.88), channel_id=1, source_target_pairs={{0,2},{1,3},{2,0},{3,1},{4,6},{5,7},{6,4},{7,5},{8,10},{9,11},{10,... | collective-permute-start | bytes 589832 | tf_op jit(solution)/shard_map/ppermute | solution.py:16
  279.2 10.0 %collective-permute-start.5 = (bf16[2,64,768]{2,1,0:T(8,128)(2,1)S(1)}, bf16[2,64,768]{2,1,0:T(8,128)(2,1)S(1)}, u32[]{:S(2)}, u32[]{:S(2)}) collective-permute-start(bf16[2,64,768]{2,1,0:T(8,128)(2,1)S(1)} %get-tuple-element.87), channel_id=1, source_target_pairs={{0,3},{1,2},{2,1},{3,0},{4,7},{5,6},{6,5},{7,4},{8,11},{9,10},{10,... | collective-permute-start | bytes 589832 | tf_op jit(solution)/shard_map/ppermute | solution.py:16
  281.6 6.2 %collective-permute-start.26 = (bf16[96,384]{1,0:T(8,128)(2,1)S(1)}, bf16[96,384]{1,0:T(8,128)(2,1)S(1)}, u32[]{:S(2)}, u32[]{:S(2)}) collective-permute-start(bf16[96,384]{1,0:T(8,128)(2,1)S(1)} %slice_bitcast_fusion.42), channel_id=1, source_target_pairs={{0,16},{4,20},{8,24},{12,28},{16,0},{20,4},{24,8},{28,12},{1,17},{... | collective-permute-start | bytes 221192 | tf_op jit(solution)/shard_map/ppermute | solution.py:16
  287.8 4.4 %collective-permute-start.27 = (bf16[96,384]{1,0:T(8,128)(2,1)S(1)}, bf16[96,384]{1,0:T(8,128)(2,1)S(1)}, u32[]{:S(2)}, u32[]{:S(2)}) collective-permute-start(bf16[96,384]{1,0:T(8,128)(2,1)S(1)} %fusion.96), channel_id=1, source_target_pairs={{0,2},{1,3},{2,0},{3,1},{4,6},{5,7},{6,4},{7,5},{8,10},{9,11},{10,... | collective-permute-start | bytes 221192 | tf_op jit(solution)/shard_map/ppermute | solution.py:16
  292.2 2.2 collective-permute-start.28
  293.0 11.6 %collective-permute-start.17 = (bf16[2,2,2,48,512]{4,3,0,1,2:T(8,128)(2,1)S(1)}, bf16[2,2,2,48,512]{4,3,0,1,2:T(8,128)(2,1)S(1)}, u32[]{:S(2)}, u32[]{:S(2)}) collective-permute-start(bf16[2,2,2,48,512]{4,3,0,1,2:T(8,128)(2,1)S(1)} %bitcast.439), channel_id=1, source_target_pairs={{0,2},{1,3},{2,0},{3,1},{4,6},{5,7},{6,4},{7,5},{8,10},{9,11},{10,... | collective-permute-start | bytes 1179656 | tf_op jit(solution)/shard_map/ppermute | solution.py:16
  294.5 14.4 %copy-start.3 = (bf16[8,384,384]{2,1,0:T(8,128)(2,1)S(1)}, bf16[8,384,384]{2,1,0:T(8,128)(2,1)}, u32[]{:S(2)}) copy-start(bf16[8,384,384]{2,1,0:T(8,128)(2,1)} %gather_fusion.7) | copy-start | bytes 7077892
  294.6 14.1 %collective-permute-start.13 = (bf16[2,2,96,640]{3,2,1,0:T(8,128)(2,1)S(1)}, bf16[2,2,96,640]{3,2,1,0:T(8,128)(2,1)S(1)}, u32[]{:S(2)}, u32[]{:S(2)}) collective-permute-start(bf16[2,2,96,640]{3,2,1,0:T(8,128)(2,1)S(1)} %slice_bitcast_fusion.4), channel_id=1, source_target_pairs={{0,4},{4,0},{8,12},{12,8},{16,20},{20,16},{24,28},{28,24},{1,5},{5... | collective-permute-start | bytes 1474568 | tf_op jit(solution)/shard_map/ppermute | solution.py:16
  304.7 15.5 %collective-permute-start.18 = (bf16[2,2,48,512]{3,2,0,1:T(8,128)(2,1)S(1)}, bf16[2,2,48,512]{3,2,0,1:T(8,128)(2,1)S(1)}, u32[]{:S(2)}, u32[]{:S(2)}) collective-permute-start(bf16[2,2,48,512]{3,2,0,1:T(8,128)(2,1)S(1)} %slice_bitcast_fusion.18), channel_id=1, source_target_pairs={{0,4},{4,0},{8,12},{12,8},{16,20},{20,16},{24,28},{28,24},{1,5},{5... | collective-permute-start | bytes 589832 | tf_op jit(solution)/shard_map/ppermute | solution.py:16
  308.9 18.0 %collective-permute-start.14 = (bf16[2,96,640]{2,1,0:T(8,128)(2,1)S(1)}, bf16[2,96,640]{2,1,0:T(8,128)(2,1)S(1)}, u32[]{:S(2)}, u32[]{:S(2)}) collective-permute-start(bf16[2,96,640]{2,1,0:T(8,128)(2,1)S(1)} %slice_bitcast_fusion.16), channel_id=1, source_target_pairs={{0,8},{4,12},{8,0},{12,4},{16,24},{20,28},{24,16},{28,20},{1,9},{5... | collective-permute-start | bytes 737288 | tf_op jit(solution)/shard_map/ppermute | solution.py:16
  317.6 36.1 %collective-permute-start.41 = (bf16[2,2,224,384]{3,2,1,0:T(8,128)(2,1)S(1)}, bf16[2,2,224,384]{3,2,1,0:T(8,128)(2,1)S(1)}, u32[]{:S(2)}, u32[]{:S(2)}) collective-permute-start(bf16[2,2,224,384]{3,2,1,0:T(8,128)(2,1)S(1)} %slice_bitcast_fusion), channel_id=1, source_target_pairs={{0,4},{4,0},{8,12},{12,8},{16,20},{20,16},{24,28},{28,24},{1,5},{5... | collective-permute-start | bytes 2064392 | tf_op jit(solution)/shard_map/ppermute | solution.py:16
  318.3 31.8 %collective-permute-start.45 = (bf16[2,2,2,80,384]{4,3,0,1,2:T(8,128)(2,1)S(1)}, bf16[2,2,2,80,384]{4,3,0,1,2:T(8,128)(2,1)S(1)}, u32[]{:S(2)}, u32[]{:S(2)}) collective-permute-start(bf16[2,2,2,80,384]{4,3,0,1,2:T(8,128)(2,1)S(1)} %bitcast.437), channel_id=1, source_target_pairs={{0,2},{1,3},{2,0},{3,1},{4,6},{5,7},{6,4},{7,5},{8,10},{9,11},{10,... | collective-permute-start | bytes 1474568 | tf_op jit(solution)/shard_map/ppermute | solution.py:16
  318.6 35.4 %collective-permute-start.30 = (bf16[2,2,96,896]{3,2,1,0:T(8,128)(2,1)S(1)}, bf16[2,2,96,896]{3,2,1,0:T(8,128)(2,1)S(1)}, u32[]{:S(2)}, u32[]{:S(2)}) collective-permute-start(bf16[2,2,96,896]{3,2,1,0:T(8,128)(2,1)S(1)} %slice_bitcast_fusion.2), channel_id=1, source_target_pairs={{0,4},{4,0},{8,12},{12,8},{16,20},{20,16},{24,28},{28,24},{1,5},{5... | collective-permute-start | bytes 2064392 | tf_op jit(solution)/shard_map/ppermute | solution.py:16
  320.3 4.7 %collective-permute-start.19 = (bf16[2,48,512]{2,1,0:T(8,128)(2,1)S(1)}, bf16[2,48,512]{2,1,0:T(8,128)(2,1)S(1)}, u32[]{:S(2)}, u32[]{:S(2)}) collective-permute-start(bf16[2,48,512]{2,1,0:T(8,128)(2,1)S(1)} %slice_bitcast_fusion.40), channel_id=1, source_target_pairs={{0,8},{4,12},{8,0},{12,4},{16,24},{20,28},{24,16},{28,20},{1,9},{5... | collective-permute-start | bytes 294920 | tf_op jit(solution)/shard_map/ppermute | solution.py:16
  325.0 25.4 %collective-permute-start.34 = (bf16[2,2,2,48,640]{4,3,0,1,2:T(8,128)(2,1)S(1)}, bf16[2,2,2,48,640]{4,3,0,1,2:T(8,128)(2,1)S(1)}, u32[]{:S(2)}, u32[]{:S(2)}) collective-permute-start(bf16[2,2,2,48,640]{4,3,0,1,2:T(8,128)(2,1)S(1)} %bitcast.438), channel_id=1, source_target_pairs={{0,2},{1,3},{2,0},{3,1},{4,6},{5,7},{6,4},{7,5},{8,10},{9,11},{10,... | collective-permute-start | bytes 1474568 | tf_op jit(solution)/shard_map/ppermute | solution.py:16
  326.9 7.3 %collective-permute-start.20 = (bf16[48,512]{1,0:T(8,128)(2,1)S(1)}, bf16[48,512]{1,0:T(8,128)(2,1)S(1)}, u32[]{:S(2)}, u32[]{:S(2)}) collective-permute-start(bf16[48,512]{1,0:T(8,128)(2,1)S(1)} %slice_bitcast_fusion.48), channel_id=1, source_target_pairs={{0,16},{4,20},{8,24},{12,28},{16,0},{20,4},{24,8},{28,12},{1,17},{... | collective-permute-start | bytes 147464 | tf_op jit(solution)/shard_map/ppermute | solution.py:16
  334.2 6.8 %collective-permute-start.15 = (bf16[96,640]{1,0:T(8,128)(2,1)S(1)}, bf16[96,640]{1,0:T(8,128)(2,1)S(1)}, u32[]{:S(2)}, u32[]{:S(2)}) collective-permute-start(bf16[96,640]{1,0:T(8,128)(2,1)S(1)} %slice_bitcast_fusion.38), channel_id=1, source_target_pairs={{0,16},{4,20},{8,24},{12,28},{16,0},{20,4},{24,8},{28,12},{1,17},{... | collective-permute-start | bytes 368648 | tf_op jit(solution)/shard_map/ppermute | solution.py:16
  341.0 4.1 collective-permute-start.21
  345.1 4.9 %collective-permute-start.16 = (bf16[96,640]{1,0:T(8,128)(2,1)S(1)}, bf16[96,640]{1,0:T(8,128)(2,1)S(1)}, u32[]{:S(2)}, u32[]{:S(2)}) collective-permute-start(bf16[96,640]{1,0:T(8,128)(2,1)S(1)} %fusion.91), channel_id=1, source_target_pairs={{0,2},{1,3},{2,0},{3,1},{4,6},{5,7},{6,4},{7,5},{8,10},{9,11},{10,... | collective-permute-start | bytes 368648 | tf_op jit(solution)/shard_map/ppermute | solution.py:16
  350.1 2.6 collective-permute-start.22
  350.3 8.8 %collective-permute-start.46 = (bf16[2,2,80,384]{3,2,0,1:T(8,128)(2,1)S(1)}, bf16[2,2,80,384]{3,2,0,1:T(8,128)(2,1)S(1)}, u32[]{:S(2)}, u32[]{:S(2)}) collective-permute-start(bf16[2,2,80,384]{3,2,0,1:T(8,128)(2,1)S(1)} %slice_bitcast_fusion.12), channel_id=1, source_target_pairs={{0,4},{4,0},{8,12},{12,8},{16,20},{20,16},{24,28},{28,24},{1,5},{5... | collective-permute-start | bytes 737288 | tf_op jit(solution)/shard_map/ppermute | solution.py:16
  350.6 13.4 %collective-permute-start.35 = (bf16[2,2,48,640]{3,2,0,1:T(8,128)(2,1)S(1)}, bf16[2,2,48,640]{3,2,0,1:T(8,128)(2,1)S(1)}, u32[]{:S(2)}, u32[]{:S(2)}) collective-permute-start(bf16[2,2,48,640]{3,2,0,1:T(8,128)(2,1)S(1)} %slice_bitcast_fusion.14), channel_id=1, source_target_pairs={{0,4},{4,0},{8,12},{12,8},{16,20},{20,16},{24,28},{28,24},{1,5},{5... | collective-permute-start | bytes 737288 | tf_op jit(solution)/shard_map/ppermute | solution.py:16
  353.9 33.3 %collective-permute-start.42 = (bf16[2,224,384]{2,1,0:T(8,128)(2,1)S(1)}, bf16[2,224,384]{2,1,0:T(8,128)(2,1)S(1)}, u32[]{:S(2)}, u32[]{:S(2)}) collective-permute-start(bf16[2,224,384]{2,1,0:T(8,128)(2,1)S(1)} %slice_bitcast_fusion.6), channel_id=1, source_target_pairs={{0,8},{4,12},{8,0},{12,4},{16,24},{20,28},{24,16},{28,20},{1,9},{5... | collective-permute-start | bytes 1032200 | tf_op jit(solution)/shard_map/ppermute | solution.py:16
  354.2 33.8 %collective-permute-start.31 = (bf16[2,96,896]{2,1,0:T(8,128)(2,1)S(1)}, bf16[2,96,896]{2,1,0:T(8,128)(2,1)S(1)}, u32[]{:S(2)}, u32[]{:S(2)}) collective-permute-start(bf16[2,96,896]{2,1,0:T(8,128)(2,1)S(1)} %slice_bitcast_fusion.8), channel_id=1, source_target_pairs={{0,8},{4,12},{8,0},{12,4},{16,24},{20,28},{24,16},{28,20},{1,9},{5... | collective-permute-start | bytes 1032200 | tf_op jit(solution)/shard_map/ppermute | solution.py:16
  359.2 15.7 %collective-permute-start.47 = (bf16[2,80,384]{2,1,0:T(8,128)(2,1)S(1)}, bf16[2,80,384]{2,1,0:T(8,128)(2,1)S(1)}, u32[]{:S(2)}, u32[]{:S(2)}) collective-permute-start(bf16[2,80,384]{2,1,0:T(8,128)(2,1)S(1)} %slice_bitcast_fusion.34), channel_id=1, source_target_pairs={{0,8},{4,12},{8,0},{12,4},{16,24},{20,28},{24,16},{28,20},{1,9},{5... | collective-permute-start | bytes 368648 | tf_op jit(solution)/shard_map/ppermute | solution.py:16
  364.1 12.4 %collective-permute-start.36 = (bf16[2,48,640]{2,1,0:T(8,128)(2,1)S(1)}, bf16[2,48,640]{2,1,0:T(8,128)(2,1)S(1)}, u32[]{:S(2)}, u32[]{:S(2)}) collective-permute-start(bf16[2,48,640]{2,1,0:T(8,128)(2,1)S(1)} %slice_bitcast_fusion.36), channel_id=1, source_target_pairs={{0,8},{4,12},{8,0},{12,4},{16,24},{20,28},{24,16},{28,20},{1,9},{5... | collective-permute-start | bytes 368648 | tf_op jit(solution)/shard_map/ppermute | solution.py:16
  375.0 6.6 %collective-permute-start.48 = (bf16[80,384]{1,0:T(8,128)(2,1)S(1)}, bf16[80,384]{1,0:T(8,128)(2,1)S(1)}, u32[]{:S(2)}, u32[]{:S(2)}) collective-permute-start(bf16[80,384]{1,0:T(8,128)(2,1)S(1)} %slice_bitcast_fusion.44), channel_id=1, source_target_pairs={{0,16},{4,20},{8,24},{12,28},{16,0},{20,4},{24,8},{28,12},{1,17},{... | collective-permute-start | bytes 184328 | tf_op jit(solution)/shard_map/ppermute | solution.py:16
  376.6 6.3 %collective-permute-start.37 = (bf16[48,640]{1,0:T(8,128)(2,1)S(1)}, bf16[48,640]{1,0:T(8,128)(2,1)S(1)}, u32[]{:S(2)}, u32[]{:S(2)}) collective-permute-start(bf16[48,640]{1,0:T(8,128)(2,1)S(1)} %slice_bitcast_fusion.46), channel_id=1, source_target_pairs={{0,16},{4,20},{8,24},{12,28},{16,0},{20,4},{24,8},{28,12},{1,17},{... | collective-permute-start | bytes 184328 | tf_op jit(solution)/shard_map/ppermute | solution.py:16
  381.6 4.3 %collective-permute-start.49 = (bf16[80,384]{1,0:T(8,128)(2,1)S(1)}, bf16[80,384]{1,0:T(8,128)(2,1)S(1)}, u32[]{:S(2)}, u32[]{:S(2)}) collective-permute-start(bf16[80,384]{1,0:T(8,128)(2,1)S(1)} %fusion.97), channel_id=1, source_target_pairs={{0,2},{1,3},{2,0},{3,1},{4,6},{5,7},{6,4},{7,5},{8,10},{9,11},{10,... | collective-permute-start | bytes 184328 | tf_op jit(solution)/shard_map/ppermute | solution.py:16
  382.9 4.3 %collective-permute-start.38 = (bf16[48,640]{1,0:T(8,128)(2,1)S(1)}, bf16[48,640]{1,0:T(8,128)(2,1)S(1)}, u32[]{:S(2)}, u32[]{:S(2)}) collective-permute-start(bf16[48,640]{1,0:T(8,128)(2,1)S(1)} %fusion.98), channel_id=1, source_target_pairs={{0,2},{1,3},{2,0},{3,1},{4,6},{5,7},{6,4},{7,5},{8,10},{9,11},{10,... | collective-permute-start | bytes 184328 | tf_op jit(solution)/shard_map/ppermute | solution.py:16
  387.2 22.9 %copy-start.31 = (bf16[48,640]{1,0:T(8,128)(2,1)}, bf16[48,640]{1,0:T(8,128)(2,1)S(1)}, u32[]{:S(2)}) copy-start(bf16[48,640]{1,0:T(8,128)(2,1)S(1)} %get-tuple-element.108) | copy-start | bytes 184324
  387.2 22.9 %copy-start.32 = (bf16[48,640]{1,0:T(8,128)(2,1)}, bf16[48,640]{1,0:T(8,128)(2,1)S(1)}, u32[]{:S(2)}) copy-start(bf16[48,640]{1,0:T(8,128)(2,1)S(1)} %get-tuple-element.109) | copy-start | bytes 184324
  387.4 13.4 %collective-permute-start.43 = (bf16[224,384]{1,0:T(8,128)(2,1)S(1)}, bf16[224,384]{1,0:T(8,128)(2,1)S(1)}, u32[]{:S(2)}, u32[]{:S(2)}) collective-permute-start(bf16[224,384]{1,0:T(8,128)(2,1)S(1)} %slice_bitcast_fusion.28), channel_id=1, source_target_pairs={{0,16},{4,20},{8,24},{12,28},{16,0},{20,4},{24,8},{28,12},{1,17},{... | collective-permute-start | bytes 516104 | tf_op jit(solution)/shard_map/ppermute | solution.py:16
  388.1 15.2 %collective-permute-start.32 = (bf16[96,896]{1,0:T(8,128)(2,1)S(1)}, bf16[96,896]{1,0:T(8,128)(2,1)S(1)}, u32[]{:S(2)}, u32[]{:S(2)}) collective-permute-start(bf16[96,896]{1,0:T(8,128)(2,1)S(1)} %slice_bitcast_fusion.30), channel_id=1, source_target_pairs={{0,16},{4,20},{8,24},{12,28},{16,0},{20,4},{24,8},{28,12},{1,17},{... | collective-permute-start | bytes 516104 | tf_op jit(solution)/shard_map/ppermute | solution.py:16
  400.9 7.0 %collective-permute-start.44 = (bf16[224,384]{1,0:T(8,128)(2,1)S(1)}, bf16[224,384]{1,0:T(8,128)(2,1)S(1)}, u32[]{:S(2)}, u32[]{:S(2)}) collective-permute-start(bf16[224,384]{1,0:T(8,128)(2,1)S(1)} %fusion.83), channel_id=1, source_target_pairs={{0,2},{1,3},{2,0},{3,1},{4,6},{5,7},{6,4},{7,5},{8,10},{9,11},{10,... | collective-permute-start | bytes 516104 | tf_op jit(solution)/shard_map/ppermute | solution.py:16
  403.4 6.7 %collective-permute-start.33 = (bf16[96,896]{1,0:T(8,128)(2,1)S(1)}, bf16[96,896]{1,0:T(8,128)(2,1)S(1)}, u32[]{:S(2)}, u32[]{:S(2)}) collective-permute-start(bf16[96,896]{1,0:T(8,128)(2,1)S(1)} %fusion.84), channel_id=1, source_target_pairs={{0,2},{1,3},{2,0},{3,1},{4,6},{5,7},{6,4},{7,5},{8,10},{9,11},{10,... | collective-permute-start | bytes 516104 | tf_op jit(solution)/shard_map/ppermute | solution.py:16
  407.9 3.6 collective-permute-start.50
  411.5 3.9 collective-permute-start.39
  (60 other events, 225.0 us)
